TPU v7x, 128 devices: a whole 4x4x4 slice. The times are simulated.
128 devices in a mesh: seq: 16 (over x_lo, z, core), head: 8 (over x_hi, y).
Axes of the slice: x: 4 (x_hi: 2, x_lo: 2; x = x_hi * 2 + x_lo), y: 4, z: 4, core: 2. Of those that a mesh axis runs over, the one named last changes fastest.
Arguments:
- queries: bfloat16 [4096, 3072], P('seq', 'head'), may hold values from -8 to 8
- keys: bfloat16 [4096, 3072], P('seq', 'head'), may hold values from -8 to 8
- values: bfloat16 [4096, 3072], P('seq', 'head'), may hold values from -6 to 6
- slide_ids: int32 [16384], P('seq'), may hold values from 0 to 15, never falling along the last dimension, each value on 1 to 10240 neighbouring positions
- head_shift_list: int32 [16], replicated, may hold values from 0 to 3
- out_weight: bfloat16 [768, 768], P('head'), may hold values from -0.625 to 0.625
- d_y: bfloat16 [16384, 768], P(('seq', 'head')), may hold values from -6 to 6
Outputs:
- layer_out: bfloat16 [16384, 768], P(('seq', 'head'))
- d_queries: bfloat16 [4096, 3072], P('seq', 'head')
- d_keys: bfloat16 [4096, 3072], P('seq', 'head')
- d_values: bfloat16 [4096, 3072], P('seq', 'head')
- d_weight: bfloat16 [768, 768], P('head')
Inputs may be any that keep to these rules, and one draw needn't show every extreme that they name: `slide_ids`: slide numbers never fall along the tokens; each slide holds 1 to 10240 tokens, and one holds exactly (10) * 1024.
All inputs are finite; a program needn't handle non-finite values.
Results may differ from a plain program's by a relative error of at most 0.012.
The roundings to bfloat16 on the way count: a program that leaves them out, or rounds other values in their place, can miss the bound.
Values may be sent and summed in bfloat16 or wider, within the bound.
A program may use at most 128 MiB of HBM per device.

v0:
```python
import functools
import math

import jax
import jax.numpy as jnp
from jax import lax
from jax.experimental import pallas as pl
from jax.experimental.pallas import tpu as pltpu
from jax.sharding import PartitionSpec as P

HEAD = 48
HALF = 64
RATE = 4
ROWS = 256
WIDTH = 768
NSEQ = 16
NHEAD = 8
SAME = 8192.0
SCALE = 1.0 / math.sqrt(HEAD)
EXP2 = SCALE * math.log2(math.e)
F32 = jnp.float32
BF16 = jnp.bfloat16


def nt(a, b):
    return lax.dot_general(a, b, (((1,), (1,)), ((), ())), preferred_element_type=F32)


def nn(a, b):
    return jnp.dot(a, b, preferred_element_type=F32)


def iota(shape, dim):
    return lax.broadcasted_iota(jnp.int32, shape, dim)


def remote(src, dst, send, recv, axis, index):
    return pltpu.make_async_remote_copy(
        src_ref=src,
        dst_ref=dst,
        send_sem=send,
        recv_sem=recv,
        device_id={axis: index},
        device_id_type=pl.DeviceIdType.MESH,
    )


def kernel(
    q_ref,
    k_ref,
    v_ref,
    id_ref,
    shift_ref,
    w_ref,
    dy_ref,
    lo_ref,
    dq_ref,
    dk_ref,
    dv_ref,
    dw_ref,
    perm,
    near_k,
    near_v,
    kv,
    q_t,
    q_n,
    qf_t,
    qf_n,
    g_t,
    g_n,
    gf_t,
    gf_n,
    e_near,
    e_far,
    top_n,
    sum_n,
    out_n,
    top_f,
    sum_f,
    out_f,
    fac_n,
    fac_f,
    delta_n,
    delta_f,
    attn_t,
    attn_n,
    attn_r,
    dys,
    ws,
    dwp,
    dwr,
    dws,
    dwf,
    gkv_s,
    gkv_r,
    acc_k,
    acc_v,
    acc_q,
    acc_qf,
    kv_send,
    kv_recv,
    dy_send,
    dy_recv,
    w_send,
    w_recv,
    at_send,
    at_recv,
    dw_send,
    dw_recv,
    df_send,
    df_recv,
    g_send,
    g_recv,
):
    seq = lax.axis_index("seq")
    head = lax.axis_index("head")

    def peer_s(i):
        return lax.rem(seq + i, NSEQ)

    def peer_h(i):
        return lax.rem(head + i, NHEAD)

    barrier = pltpu.get_barrier_semaphore()

    @pl.loop(1, NSEQ)
    def _(i):
        pl.semaphore_signal(
            barrier, inc=1, device_id={"seq": peer_s(i)}, device_id_type=pl.DeviceIdType.MESH
        )

    @pl.loop(1, NHEAD)
    def _(i):
        pl.semaphore_signal(
            barrier, inc=1, device_id={"head": peer_h(i)}, device_id_type=pl.DeviceIdType.MESH
        )

    row = iota((4 * 128, 384), 0)
    col = iota((4 * 128, 384), 1)
    lane = lax.rem(row, 128)
    within = lax.rem(lane, HALF)
    source = (lane // HALF) * (RATE * HEAD) + (row // 128) * HEAD + within
    perm[...] = jnp.where((within < HEAD) & (source == col), 1.0, 0.0).astype(BF16)

    slide_col = lax.rem(iota((128, 128), 0), HALF) - HEAD
    below = jnp.zeros((128, 128), F32)
    upto = jnp.zeros((128, 128), F32)
    for s in range(8):
        ids = id_ref[s : s + 1, :]
        below = below + jnp.where(ids < slide_col, 1.0, 0.0)
        upto = upto + jnp.where(ids <= slide_col, 1.0, 0.0)
    ones = jnp.ones((8, 128), BF16)
    first_row = nt(ones, below.astype(BF16))[0:1, :]
    last_row = nt(ones, upto.astype(BF16))[0:1, :]
    first_col = jnp.sum(below, axis=1, keepdims=True)
    last_col = jnp.sum(upto, axis=1, keepdims=True)

    shift0 = shift_ref[2 * head]
    shift1 = shift_ref[2 * head + 1]
    lane_row = iota((1, 128), 1)
    lane_col = iota((128, 1), 0)
    shift_row = jnp.where(lane_row < HALF, shift0, shift1)
    shift_col = jnp.where(lane_col < HALF, shift0, shift1)
    hot_row = lax.rem(lane_row, HALF) >= HEAD
    hot_col = lax.rem(lane_col, HALF) >= HEAD
    shift_q = [jnp.full((1, ROWS), shift0, jnp.int32), jnp.full((1, ROWS), shift1, jnp.int32)]

    k_p = nt(k_ref[...], perm[...])
    v_p = nt(v_ref[...], perm[...])
    far_k = jnp.zeros((ROWS, 128), F32)
    far_v = jnp.zeros((ROWS, 128), F32)
    for r in range(RATE):
        at = (iota((ROWS, 128), 0) * RATE + r).astype(F32)
        hot = jnp.where(hot_row & (at >= first_row) & (at < last_row), 1.0, 0.0)
        k_r = k_p[:, r * 128 : (r + 1) * 128] + hot
        v_r = v_p[:, r * 128 : (r + 1) * 128]
        near_k[r] = k_r.astype(BF16)
        near_v[r] = v_r.astype(BF16)
        far_k = jnp.where(shift_row == r, k_r, far_k)
        far_v = jnp.where(shift_row == r, v_r, far_v)
    kv[seq, 0] = far_k.astype(BF16)
    kv[seq, 1] = far_v.astype(BF16)

    rm_row = iota((128, 128), 0)
    rm_col = iota((128, 128), 1)
    to_rm = jnp.where(rm_col == lax.rem(rm_row, 32) * RATE + rm_row // 32, 1.0, 0.0).astype(BF16)
    dy_own = nn(to_rm, dy_ref[...]).astype(BF16)
    own_rows = pl.ds(pl.multiple_of(head * 32, 32), 32)
    for r in range(RATE):
        dys[r, own_rows, :] = dy_own[r * 32 : (r + 1) * 32]

    zeros16 = jnp.zeros((16, WIDTH), BF16)

    ws[head, 0:48] = w_ref[0:48]
    ws[head, 48:64] = zeros16
    ws[head, 64:112] = w_ref[48:96]
    for h in range(NHEAD):
        ws[h, 112:128] = zeros16

    pl.semaphore_wait(barrier, NSEQ - 1 + NHEAD - 1)

    def kv_copy(slot, i):
        return remote(kv.at[slot], kv.at[slot], kv_send.at[i], kv_recv.at[slot], "seq", peer_s(i))

    def dy_copy(owner, i):
        rows = pl.ds(pl.multiple_of(owner * 32, 32), 32)
        part = dys.at[:, rows, :]
        return remote(part, part, dy_send.at[i], dy_recv.at[owner], "head", peer_h(i))

    def w_copy(owner, i):
        part = ws.at[owner, 0:112]
        return remote(part, part, w_send.at[i], w_recv.at[owner], "head", peer_h(i))

    @pl.loop(1, NSEQ)
    def _(i):
        kv_copy(seq, i).start()

    @pl.loop(1, NHEAD)
    def _(i):
        dy_copy(head, i).start()

    @pl.loop(1, NHEAD)
    def _(i):
        w_copy(head, i).start()

    q_p = nt(q_ref[...], perm[...])
    q_pt = nt(perm[...], q_ref[...])
    far_q = jnp.zeros((ROWS, 128), F32)
    far_qt = jnp.zeros((128, ROWS), F32)
    for r in range(RATE):
        at = (iota((128, ROWS), 1) * RATE + r).astype(F32)
        hot = jnp.where(hot_col & (at >= first_col) & (at < last_col), SAME, 0.0)
        q_r = q_p[:, r * 128 : (r + 1) * 128]
        q_rt = q_pt[r * 128 : (r + 1) * 128, :] + hot
        q_n[0, r] = jnp.where(lane_row < HALF, q_r, 0.0).astype(BF16)
        q_n[1, r] = jnp.where(lane_row < HALF, 0.0, q_r).astype(BF16)
        q_t[0, r] = jnp.where(lane_col < HALF, q_rt, 0.0).astype(BF16)
        q_t[1, r] = jnp.where(lane_col < HALF, 0.0, q_rt).astype(BF16)
        far_q = jnp.where(shift_row == r, q_r, far_q)
        far_qt = jnp.where(shift_col == r, q_rt, far_qt)
    qf_n[0] = jnp.where(lane_row < HALF, far_q, 0.0).astype(BF16)
    qf_n[1] = jnp.where(lane_row < HALF, 0.0, far_q).astype(BF16)
    qf_t[0] = jnp.where(lane_col < HALF, far_qt, 0.0).astype(BF16)
    qf_t[1] = jnp.where(lane_col < HALF, 0.0, far_qt).astype(BF16)

    def forward(keys, vals, q_of, e_of, h):
        top = None
        for b in range(4):
            s = nn(keys(b), q_of)
            e_of[b] = s
            m = jnp.max(s, axis=0, keepdims=True)
            top = m if top is None else jnp.maximum(top, m)
        total = jnp.zeros((1, ROWS), F32)
        out = jnp.zeros((HALF, ROWS), F32)
        for b in range(4):
            e = jnp.exp2((e_of[b] - top) * EXP2)
            e_of[b] = e
            total = total + jnp.sum(e, axis=0, keepdims=True)
            v_t = vals(b).T[h * HALF : (h + 1) * HALF]
            out = out + nn(v_t, e.astype(BF16))
        return top, total, out

    @pl.loop(0, RATE)
    def _(r):
        for h in range(2):
            top, total, out = forward(
                lambda b: near_k[b], lambda b: near_v[b], q_t[h, r], e_near.at[h, r], h
            )
            top_n[h, r] = top
            sum_n[h, r] = total
            out_n[h, r] = out

    group = seq // 4

    @pl.loop(0, 4)
    def _(i):
        g = lax.rem(group + i, 4)
        for b in range(4):

            @pl.when(g * 4 + b != seq)
            def _():
                kv_copy(g * 4 + b, 1).wait_recv()

        for h in range(2):
            top, total, out = forward(
                lambda b: kv[g * 4 + b, 0], lambda b: kv[g * 4 + b, 1], qf_t[h], e_far.at[h, g], h
            )
            top_f[h, g] = top
            sum_f[h, g] = total
            out_f[h, g] = out

    for h in range(2):
        half = slice(h * HALF, (h + 1) * HALF)
        far_top = top_f[h, 0]
        for g in range(1, 4):
            far_top = jnp.maximum(far_top, top_f[h, g])
        sel_top = top_n[h, 0]
        for r in range(1, RATE):
            sel_top = jnp.where(shift_q[h] == r, top_n[h, r], sel_top)
        sel_top = jnp.maximum(sel_top, far_top)
        far_total = jnp.zeros((1, ROWS), F32)
        far_out = jnp.zeros((HALF, ROWS), F32)
        weights = []
        for g in range(4):
            weight = jnp.exp2((top_f[h, g] - sel_top) * EXP2)
            weights.append(weight)
            far_total = far_total + weight * sum_f[h, g]
            far_out = far_out + weight * out_f[h, g]
        far_inv = jnp.zeros((1, ROWS), F32)
        for r in range(RATE):
            mine = shift_q[h] == r
            top = jnp.where(mine, sel_top, top_n[h, r])
            weight = jnp.exp2((top_n[h, r] - top) * EXP2)
            total = weight * sum_n[h, r] + jnp.where(mine, far_total, 0.0)
            inverse = 1.0 / total
            fac_n[h, r] = weight * inverse
            far_inv = jnp.where(mine, inverse, far_inv)
            out = weight * out_n[h, r] + jnp.where(mine, far_out, 0.0)
            attn_t[r, half] = (out * inverse).astype(BF16)
        for g in range(4):
            fac_f[h, g] = weights[g] * far_inv

    for r in range(RATE):
        attn_n[r] = attn_t[r].astype(F32).T.astype(BF16)

    def at_copy(slot, i):
        rows = pl.ds(pl.multiple_of(peer_h(i) * 32, 32), 32)
        return remote(
            attn_n.at[:, rows, :], attn_r.at[slot], at_send.at[i], at_recv.at[slot], "head", peer_h(i)
        )

    @pl.loop(1, NHEAD)
    def _(i):
        at_copy(head, i).start()

    for r in range(RATE):
        attn_r[head, r] = attn_n[r, own_rows, :]

    @pl.loop(1, NHEAD)
    def _(i):
        dy_copy(peer_h(i), i).wait_recv()

    w_own = ws[head]
    far_g = jnp.zeros((ROWS, 128), F32)
    far_gt = jnp.zeros((128, ROWS), F32)
    weight_grad = jnp.zeros((128, WIDTH), F32)
    far_d = [jnp.zeros((1, ROWS), F32), jnp.zeros((1, ROWS), F32)]
    for r in range(RATE):
        g_r = nt(dys[r], w_own)
        g_rt = nt(w_own, dys[r])
        weight_grad = weight_grad + nn(attn_t[r], dys[r])
        g_n[0, r] = jnp.where(lane_row < HALF, g_r, 0.0).astype(BF16)
        g_n[1, r] = jnp.where(lane_row < HALF, 0.0, g_r).astype(BF16)
        g_t[0, r] = jnp.where(lane_col < HALF, g_rt, 0.0).astype(BF16)
        g_t[1, r] = jnp.where(lane_col < HALF, 0.0, g_rt).astype(BF16)
        far_g = jnp.where(shift_row == r, g_r, far_g)
        far_gt = jnp.where(shift_col == r, g_rt, far_gt)
        product = g_rt.astype(BF16).astype(F32) * attn_t[r].astype(F32)
        for h in range(2):
            half = slice(h * HALF, (h + 1) * HALF)
            d = jnp.sum(product[half], axis=0, keepdims=True)
            delta_n[h, r] = d
            far_d[h] = jnp.where(shift_q[h] == r, d, far_d[h])
    gf_n[0] = jnp.where(lane_row < HALF, far_g, 0.0).astype(BF16)
    gf_n[1] = jnp.where(lane_row < HALF, 0.0, far_g).astype(BF16)
    gf_t[0] = jnp.where(lane_col < HALF, far_gt, 0.0).astype(BF16)
    gf_t[1] = jnp.where(lane_col < HALF, 0.0, far_gt).astype(BF16)
    delta_f[0] = far_d[0]
    delta_f[1] = far_d[1]

    for j in range(NSEQ):
        dwp[j] = weight_grad[j * 8 : (j + 1) * 8]
    dwr[seq] = dwp[seq]

    def dw_copy(slot, i):
        return remote(
            dwp.at[peer_s(i)], dwr.at[slot], dw_send.at[i], dw_recv.at[slot], "seq", peer_s(i)
        )

    @pl.loop(1, NSEQ)
    def _(i):
        dw_copy(seq, i).start()

    def backward(keys, vals, g_tr, g_na, q_na, e_of, factor, delta, put):
        dq = [jnp.zeros((HALF, ROWS), F32), jnp.zeros((HALF, ROWS), F32)]
        for b in range(4):
            k_t = keys(b).T
            val = vals(b)
            dk = jnp.zeros((ROWS, 128), F32)
            dv = jnp.zeros((ROWS, 128), F32)
            for h in range(2):
                p = e_of(h)[b] * factor(h)
                ds = (p * (nn(val, g_tr(h)) - delta(h))).astype(BF16)
                dv = dv + nn(p.astype(BF16), g_na(h))
                dk = dk + nn(ds, q_na(h))
                dq[h] = dq[h] + nn(k_t[h * HALF : (h + 1) * HALF], ds)
            put(b, dk, dv)
        return dq

    def grad_copy(slot, dst):
        return remote(
            gkv_s.at[dst], gkv_r.at[slot], g_send.at[dst], g_recv.at[slot], "seq", dst
        )

    acc_qf[...] = jnp.zeros((128, ROWS), F32)

    @pl.loop(0, 4)
    def _(i):
        g = lax.rem(group + 1 + i, 4)

        def put(b, dk, dv):
            dst = g * 4 + b
            gkv_s[dst, 0] = dk.astype(BF16)
            gkv_s[dst, 1] = dv.astype(BF16)

            @pl.when(dst != seq)
            def _():
                grad_copy(seq, dst).start()

        dq = backward(
            lambda b: kv[g * 4 + b, 0],
            lambda b: kv[g * 4 + b, 1],
            lambda h: gf_t[h],
            lambda h: gf_n[h],
            lambda h: qf_n[h],
            lambda h: e_far.at[h, g],
            lambda h: fac_f[h, g],
            lambda h: delta_f[h],
            put,
        )
        for h in range(2):
            half = slice(h * HALF, (h + 1) * HALF)
            acc_qf[half] = acc_qf[half] + dq[h]

    @pl.loop(1, NSEQ)
    def _(i):
        dw_copy(peer_s(i), i).wait_recv()

    part = dwr[0]
    for j in range(1, NSEQ):
        part = part + dwr[j]
    dws[...] = part
    dwf[seq] = part

    def df_copy(slot, i):
        return remote(dws, dwf.at[slot], df_send.at[i], df_recv.at[slot], "seq", peer_s(i))

    @pl.loop(1, NSEQ)
    def _(i):
        df_copy(seq, i).start()

    acc_k[...] = jnp.zeros((4, ROWS, 128), F32)
    acc_v[...] = jnp.zeros((4, ROWS, 128), F32)

    @pl.loop(0, RATE)
    def _(r):
        def put(b, dk, dv):
            acc_k[b] = acc_k[b] + dk
            acc_v[b] = acc_v[b] + dv

        dq = backward(
            lambda b: near_k[b],
            lambda b: near_v[b],
            lambda h: g_t[h, r],
            lambda h: g_n[h, r],
            lambda h: q_n[h, r],
            lambda h: e_near.at[h, r],
            lambda h: fac_n[h, r],
            lambda h: delta_n[h, r],
            put,
        )
        for h in range(2):
            acc_q[r, h * HALF : (h + 1) * HALF] = dq[h]

    dq_parts = []
    for r in range(RATE):
        dq_r = (acc_q[r] + jnp.where(shift_col == r, acc_qf[...], 0.0)) * SCALE
        dq_parts.append(dq_r.T.astype(BF16))
    dq_ref[...] = nn(jnp.concatenate(dq_parts, axis=1), perm[...]).astype(BF16)

    @pl.loop(1, NHEAD)
    def _(i):
        w_copy(peer_h(i), i).wait_recv()
        at_copy(peer_h(i), i).wait_recv()

    from_rm = jnp.where(rm_row == lax.rem(rm_col, 32) * RATE + rm_col // 32, 1.0, 0.0).astype(BF16)
    result = jnp.zeros((128, WIDTH), F32)
    for h in range(NHEAD):
        rows = nn(from_rm, attn_r[h].reshape(128, 128)).astype(BF16)
        result = result + nn(rows, ws[h])
    lo_ref[...] = result.astype(BF16)

    @pl.loop(1, NSEQ)
    def _(i):
        grad_copy(peer_s(i), peer_s(i)).wait_recv()

    gkv_r[seq] = gkv_s[seq]
    sum_k = gkv_r[0, 0].astype(F32)
    sum_v = gkv_r[0, 1].astype(F32)
    for j in range(1, NSEQ):
        sum_k = sum_k + gkv_r[j, 0].astype(F32)
        sum_v = sum_v + gkv_r[j, 1].astype(F32)
    dk_parts = []
    dv_parts = []
    for r in range(RATE):
        mine = shift_row == r
        dk_parts.append(((acc_k[r] + jnp.where(mine, sum_k, 0.0)) * SCALE).astype(BF16))
        dv_parts.append((acc_v[r] + jnp.where(mine, sum_v, 0.0)).astype(BF16))
    dk_ref[...] = nn(jnp.concatenate(dk_parts, axis=1), perm[...]).astype(BF16)
    dv_ref[...] = nn(jnp.concatenate(dv_parts, axis=1), perm[...]).astype(BF16)

    @pl.loop(1, NSEQ)
    def _(i):
        df_copy(peer_s(i), i).wait_recv()

    whole = dwf[...].reshape(128, WIDTH)
    dw_ref[0:48] = whole[0:48].astype(BF16)
    dw_ref[48:96] = whole[64:112].astype(BF16)

    @pl.loop(1, NSEQ)
    def _(i):
        kv_copy(seq, i).wait_send()
        dw_copy(seq, i).wait_send()
        df_copy(seq, i).wait_send()
        grad_copy(seq, peer_s(i)).wait_send()

    @pl.loop(1, NHEAD)
    def _(i):
        dy_copy(head, i).wait_send()
        w_copy(head, i).wait_send()
        at_copy(head, i).wait_send()


def body(queries, keys, values, slide_ids, head_shift_list, out_weight, d_y):
    vmem = pl.BlockSpec(memory_space=pltpu.VMEM)
    smem = pl.BlockSpec(memory_space=pltpu.SMEM)
    sems = pltpu.SemaphoreType.DMA
    return pl.pallas_call(
        kernel,
        out_shape=(
            jax.ShapeDtypeStruct((128, WIDTH), BF16),
            jax.ShapeDtypeStruct((ROWS, 384), BF16),
            jax.ShapeDtypeStruct((ROWS, 384), BF16),
            jax.ShapeDtypeStruct((ROWS, 384), BF16),
            jax.ShapeDtypeStruct((96, WIDTH), BF16),
        ),
        in_specs=[vmem, vmem, vmem, vmem, smem, vmem, vmem],
        out_specs=(vmem,) * 5,
        scratch_shapes=[
            pltpu.VMEM((4 * 128, 384), BF16),
            pltpu.VMEM((4, ROWS, 128), BF16),
            pltpu.VMEM((4, ROWS, 128), BF16),
            pltpu.VMEM((NSEQ, 2, ROWS, 128), BF16),
            pltpu.VMEM((2, RATE, 128, ROWS), BF16),
            pltpu.VMEM((2, RATE, ROWS, 128), BF16),
            pltpu.VMEM((2, 128, ROWS), BF16),
            pltpu.VMEM((2, ROWS, 128), BF16),
            pltpu.VMEM((2, RATE, 128, ROWS), BF16),
            pltpu.VMEM((2, RATE, ROWS, 128), BF16),
            pltpu.VMEM((2, 128, ROWS), BF16),
            pltpu.VMEM((2, ROWS, 128), BF16),
            pltpu.VMEM((2, RATE, 4, ROWS, ROWS), F32),
            pltpu.VMEM((2, 4, 4, ROWS, ROWS), F32),
            pltpu.VMEM((2, RATE, 1, ROWS), F32),
            pltpu.VMEM((2, RATE, 1, ROWS), F32),
            pltpu.VMEM((2, RATE, HALF, ROWS), F32),
            pltpu.VMEM((2, 4, 1, ROWS), F32),
            pltpu.VMEM((2, 4, 1, ROWS), F32),
            pltpu.VMEM((2, 4, HALF, ROWS), F32),
            pltpu.VMEM((2, RATE, 1, ROWS), F32),
            pltpu.VMEM((2, 4, 1, ROWS), F32),
            pltpu.VMEM((2, RATE, 1, ROWS), F32),
            pltpu.VMEM((2, 1, ROWS), F32),
            pltpu.VMEM((RATE, 128, ROWS), BF16),
            pltpu.VMEM((RATE, ROWS, 128), BF16),
            pltpu.VMEM((NHEAD, RATE, 32, 128), BF16),
            pltpu.VMEM((RATE, ROWS, WIDTH), BF16),
            pltpu.VMEM((NHEAD, 128, WIDTH), BF16),
            pltpu.VMEM((NSEQ, 8, WIDTH), F32),
            pltpu.VMEM((NSEQ, 8, WIDTH), F32),
            pltpu.VMEM((8, WIDTH), F32),
            pltpu.VMEM((NSEQ, 8, WIDTH), F32),
            pltpu.VMEM((NSEQ, 2, ROWS, 128), BF16),
            pltpu.VMEM((NSEQ, 2, ROWS, 128), BF16),
            pltpu.VMEM((4, ROWS, 128), F32),
            pltpu.VMEM((4, ROWS, 128), F32),
            pltpu.VMEM((RATE, 128, ROWS), F32),
            pltpu.VMEM((128, ROWS), F32),
            sems((NSEQ,)),
            sems((NSEQ,)),
            sems((NHEAD,)),
            sems((NHEAD,)),
            sems((NHEAD,)),
            sems((NHEAD,)),
            sems((NHEAD,)),
            sems((NHEAD,)),
            sems((NSEQ,)),
            sems((NSEQ,)),
            sems((NSEQ,)),
            sems((NSEQ,)),
            sems((NSEQ,)),
            sems((NSEQ,)),
        ],
        compiler_params=pltpu.CompilerParams(
            collective_id=0, has_side_effects=True, vmem_limit_bytes=56 * 1024 * 1024
        ),
        cost_estimate=pl.CostEstimate(
            flops=3_000_000_000, bytes_accessed=4_000_000, transcendentals=5_000_000
        ),
    )(
        queries,
        keys,
        values,
        slide_ids.reshape(8, 128),
        head_shift_list,
        out_weight,
        d_y,
    )


def solution(mesh):
    placed = (
        P("seq", "head"),
        P("seq", "head"),
        P("seq", "head"),
        P("seq"),
        P(),
        P("head", None),
        P(("seq", "head"), None),
    )
    return jax.shard_map(
        body,
        mesh=mesh,
        in_specs=placed,
        out_specs=(
            P(("seq", "head"), None),
            P("seq", "head"),
            P("seq", "head"),
            P("seq", "head"),
            P("head", None),
        ),
        check_vma=False,
    )
```

profile of v0, /device:TPU:125, one launch (start us, length us, event | category | flops | bytes accessed | tf_op | source)
XLA Modules:
  0.0 123.3 jit_solution(15906898474056872925)
XLA Ops:
  0.6 117.4 %shard_map.110 = (bf16[128,768]{1,0:T(8,128)(2,1)}, bf16[256,384]{1,0:T(8,128)(2,1)}, bf16[256,384]{1,0:T(8,128)(2,1)}, bf16[256,384]{1,0:T(8,128)(2,1)}, bf16[96,768]{1,0:T(8,128)(2,1)}) custom-call(bf16[256,384]{1,0:T(8,128)(2,1)} %q_ref.1, bf16[256,384]{1,0:T(8,128)(2,1)} %k_ref.1, bf16[256,384]{1,0:T(8,128)(2,1)} %v_ref.1, s32[8,128]{1,0:T(8,128)} %bitcast.1, ...), custom_call_target="tpu_custom_call" | custom-call | flops 3000000000 | bytes 4000000 | tf_op jit(solution)/shard_map/pallas_call | solution.py:538
  118.0 0.0 copy-start.2
  118.0 1.7 %copy.17 = bf16[128,768]{1,0:T(8,128)(2,1)} copy(bf16[128,768]{1,0:T(8,128)(2,1)} %get-tuple-element.10) | data formatting | bytes 393216
  119.7 0.0 copy-done.2
  119.7 0.0 copy-start.1
  119.7 0.7 copy.18
  120.3 0.3 copy-done.1
  120.7 0.0 copy-start
  120.7 0.7 copy.19
  121.3 0.3 copy-done
  121.7 0.0 copy-start.3
  121.7 0.7 copy.20
  122.3 0.3 copy-done.3
  122.6 0.7 copy.21
Async XLA Ops:
  118.0 1.7 %copy-start.2 = (bf16[256,384]{1,0:T(8,128)(2,1)S(1)}, bf16[256,384]{1,0:T(8,128)(2,1)}, u32[]{:S(2)}) copy-start(bf16[256,384]{1,0:T(8,128)(2,1)} %get-tuple-element.11) | copy-start | bytes 589828
  119.7 1.0 copy-start.1
  120.7 1.0 copy-start
  121.7 1.0 copy-start.3
where the time goes:
time: 124 us; the launch traced here: 123 us
  Pallas kernels  117 us (94%)
  local copies, waits for them, and re-layouts  5.29 us (4%)
    pallas_call x1, Pallas kernels, body(): pl.pallas_call(kernel, out_shape=(jax.ShapeDtypeStruct((128, WIDTH), BF16...  117 us
    unnamed x13, local copies, waits for them, and re-layouts  5.29 us

commit v1 on v0

--- a/solution.py
+++ b/solution.py
@@ -88,10 +88,12 @@
     dys,
     ws,
     dwp,
+    dwx,
+    dwm,
     dwr,
-    dws,
     dwf,
     gkv_s,
+    gkv_x,
     gkv_r,
     acc_k,
     acc_v,
@@ -103,34 +105,61 @@
     dy_recv,
     w_send,
     w_recv,
+    ws_send,
+    ws_recv,
     at_send,
     at_recv,
+    dx_sem,
     dw_send,
     dw_recv,
     df_send,
     df_recv,
+    dc_sem,
+    gx_send,
+    gx_recv,
     g_send,
     g_recv,
 ):
     seq = lax.axis_index("seq")
     head = lax.axis_index("head")
 
-    def peer_s(i):
-        return lax.rem(seq + i, NSEQ)
+    x_lo, z, core = seq // 8, lax.rem(seq // 2, 4), lax.rem(seq, 2)
+    x_hi, y = head // 4, lax.rem(head, 4)
+    chip = seq // 2
+
+    def at_chip(j):
+        return j * 2 + core
+
+    def in_seq(x, dz, c):
+        return x * 8 + lax.rem(z + dz, 4) * 2 + c
+
+    def in_head(x, dy):
+        return x * 4 + lax.rem(y + dy, 4)
+
+    def peer_c(i):
+        return lax.rem(chip + i, 8)
 
     def peer_h(i):
         return lax.rem(head + i, NHEAD)
 
+    sibling = in_seq(x_lo, 0, 1 - core)
+    partner = in_seq(1 - x_lo, 0, core)
+    partner_h = in_head(1 - x_hi, 0)
+    turns = (1, 3, 2)
+
     barrier = pltpu.get_barrier_semaphore()
-
-    @pl.loop(1, NSEQ)
+    pl.semaphore_signal(
+        barrier, inc=1, device_id={"seq": sibling}, device_id_type=pl.DeviceIdType.MESH
+    )
+
+    @pl.loop(1, 8)
     def _(i):
         pl.semaphore_signal(
-            barrier, inc=1, device_id={"seq": peer_s(i)}, device_id_type=pl.DeviceIdType.MESH
+            barrier,
+            inc=1,
+            device_id={"seq": at_chip(peer_c(i))},
+            device_id_type=pl.DeviceIdType.MESH,
         )
-
-    @pl.loop(1, NHEAD)
-    def _(i):
         pl.semaphore_signal(
             barrier, inc=1, device_id={"head": peer_h(i)}, device_id_type=pl.DeviceIdType.MESH
         )
@@ -192,36 +221,36 @@
     zeros16 = jnp.zeros((16, WIDTH), BF16)
 
     ws[head, 0:48] = w_ref[0:48]
-    ws[head, 48:64] = zeros16
     ws[head, 64:112] = w_ref[48:96]
     for h in range(NHEAD):
+        ws[h, 48:64] = zeros16
         ws[h, 112:128] = zeros16
 
-    pl.semaphore_wait(barrier, NSEQ - 1 + NHEAD - 1)
-
-    def kv_copy(slot, i):
-        return remote(kv.at[slot], kv.at[slot], kv_send.at[i], kv_recv.at[slot], "seq", peer_s(i))
-
-    def dy_copy(owner, i):
+    pl.semaphore_wait(barrier, 15)
+
+    def kv_copy(slot, i, dst):
+        return remote(kv.at[slot], kv.at[slot], kv_send.at[i], kv_recv.at[slot], "seq", dst)
+
+    def dy_copy(owner, i, dst):
         rows = pl.ds(pl.multiple_of(owner * 32, 32), 32)
         part = dys.at[:, rows, :]
-        return remote(part, part, dy_send.at[i], dy_recv.at[owner], "head", peer_h(i))
+        return remote(part, part, dy_send.at[i], dy_recv.at[owner], "head", dst)
 
     def w_copy(owner, i):
-        part = ws.at[owner, 0:112]
+        part = ws.at[owner, pl.ds(pl.multiple_of(core * HALF, HALF), HEAD)]
         return remote(part, part, w_send.at[i], w_recv.at[owner], "head", peer_h(i))
 
-    @pl.loop(1, NSEQ)
-    def _(i):
-        kv_copy(seq, i).start()
-
-    @pl.loop(1, NHEAD)
-    def _(i):
-        dy_copy(head, i).start()
-
-    @pl.loop(1, NHEAD)
-    def _(i):
-        w_copy(head, i).start()
+    def w_share(owner, half):
+        part = ws.at[owner, pl.ds(pl.multiple_of(half * HALF, HALF), HEAD)]
+        return remote(part, part, ws_send.at[owner], ws_recv.at[owner], "seq", sibling)
+
+    kv_copy(seq, 0, partner).start()
+    for j, turn in enumerate(turns):
+        kv_copy(seq, 1 + j, in_seq(x_lo, turn, core)).start()
+    kv_copy(seq, 4, sibling).start()
+    dy_copy(head, 0, partner_h).start()
+    for j, turn in enumerate(turns):
+        dy_copy(head, 1 + j, in_head(x_hi, turn)).start()
 
     q_p = nt(q_ref[...], perm[...])
     q_pt = nt(perm[...], q_ref[...])
@@ -270,24 +299,58 @@
             sum_n[h, r] = total
             out_n[h, r] = out
 
-    group = seq // 4
+        @pl.when(r == 0)
+        def _():
+            kv_copy(partner, 0, partner).wait_recv()
+            for j, turn in enumerate(turns):
+                kv_copy(partner, 5 + j, in_seq(x_lo, turn, core)).start()
+            kv_copy(partner, 8, sibling).start()
+
+        @pl.when(r == 1)
+        def _():
+            dy_copy(partner_h, 0, partner_h).wait_recv()
+            for j, turn in enumerate(turns):
+                dy_copy(partner_h, 4 + j, in_head(x_hi, turn)).start()
+
+    def share(i):
+        dz = i + i // 2 - 2 * (i // 3)
+        for x in range(2):
+            slot = in_seq(x, dz, core)
+            kv_copy(slot, 0, partner).wait_recv()
+            kv_copy(slot, 9 + 2 * (i - 1) + x, sibling).start()
+
+    def w_start():
+        @pl.loop(1, NHEAD)
+        def _(i):
+            w_copy(head, i).start()
 
     @pl.loop(0, 4)
     def _(i):
-        g = lax.rem(group + i, 4)
-        for b in range(4):
-
-            @pl.when(g * 4 + b != seq)
-            def _():
-                kv_copy(g * 4 + b, 1).wait_recv()
+        dz = i + i // 2 - 2 * (i // 3)
+
+        @pl.when(i == 1)
+        def _():
+            share(1)
+            w_start()
+
+        @pl.when((i == 1) | (i == 2))
+        def _():
+            share(i + 1)
+
+        for x in range(2):
+            kv_copy(in_seq(x, dz, 1 - core), 0, partner).wait_recv()
 
         for h in range(2):
             top, total, out = forward(
-                lambda b: kv[g * 4 + b, 0], lambda b: kv[g * 4 + b, 1], qf_t[h], e_far.at[h, g], h
+                lambda b: kv[in_seq(b // 2, dz, b % 2), 0],
+                lambda b: kv[in_seq(b // 2, dz, b % 2), 1],
+                qf_t[h],
+                e_far.at[h, i],
+                h,
             )
-            top_f[h, g] = top
-            sum_f[h, g] = total
-            out_f[h, g] = out
+            top_f[h, i] = top
+            sum_f[h, i] = total
+            out_f[h, i] = out
 
     for h in range(2):
         half = slice(h * HALF, (h + 1) * HALF)
@@ -336,9 +399,9 @@
     for r in range(RATE):
         attn_r[head, r] = attn_n[r, own_rows, :]
 
-    @pl.loop(1, NHEAD)
-    def _(i):
-        dy_copy(peer_h(i), i).wait_recv()
+    for turn in turns:
+        for x in range(2):
+            dy_copy(in_head(x, turn), 0, partner_h).wait_recv()
 
     w_own = ws[head]
     far_g = jnp.zeros((ROWS, 128), F32)
@@ -368,18 +431,25 @@
     delta_f[0] = far_d[0]
     delta_f[1] = far_d[1]
 
-    for j in range(NSEQ):
-        dwp[j] = weight_grad[j * 8 : (j + 1) * 8]
-    dwr[seq] = dwp[seq]
+    for half in range(2):
+        for j in range(8):
+            dwp[half, j] = weight_grad[j * 16 : (j + 1) * 16, half * 384 : (half + 1) * 384]
+
+    def dx_copy(half):
+        return remote(dwp.at[half], dwx, dx_sem.at[0], dx_sem.at[1], "seq", sibling)
 
     def dw_copy(slot, i):
-        return remote(
-            dwp.at[peer_s(i)], dwr.at[slot], dw_send.at[i], dw_recv.at[slot], "seq", peer_s(i)
-        )
-
-    @pl.loop(1, NSEQ)
-    def _(i):
-        dw_copy(seq, i).start()
+        dst = peer_c(i)
+        return remote(dwm.at[dst], dwr.at[slot], dw_send.at[i], dw_recv.at[slot], "seq", at_chip(dst))
+
+    def df_copy(slot, i):
+        part = dwf.at[core, slot]
+        return remote(part, part, df_send.at[i], df_recv.at[slot], "seq", at_chip(peer_c(i)))
+
+    def dc_copy(half):
+        return remote(dwf.at[half], dwf.at[half], dc_sem.at[0], dc_sem.at[1], "seq", sibling)
+
+    dx_copy(1 - core).start()
 
     def backward(keys, vals, g_tr, g_na, q_na, e_of, factor, delta, put):
         dq = [jnp.zeros((HALF, ROWS), F32), jnp.zeros((HALF, ROWS), F32)]
@@ -397,34 +467,54 @@
             put(b, dk, dv)
         return dq
 
-    def grad_copy(slot, dst):
+    def gx_copy(slot):
         return remote(
-            gkv_s.at[dst], gkv_r.at[slot], g_send.at[dst], g_recv.at[slot], "seq", dst
+            gkv_s.at[slot], gkv_x.at[slot], gx_send.at[slot], gx_recv.at[slot], "seq", sibling
         )
 
+    def grad_copy(slot, sender, dst):
+        return remote(
+            gkv_s.at[slot], gkv_r.at[sender], g_send.at[slot // 2], g_recv.at[sender], "seq", dst
+        )
+
+    def merge(i):
+        dz = i + i // 2 - 2 * (i // 3)
+        for x in range(2):
+            slot = in_seq(x, dz, core)
+            gx_copy(slot).wait_recv()
+            for j in range(2):
+                gkv_s[slot, j] = (
+                    gkv_s[slot, j].astype(F32) + gkv_x[slot, j].astype(F32)
+                ).astype(BF16)
+
+            @pl.when(slot != seq)
+            def _():
+                grad_copy(slot, chip, slot).start()
+
     acc_qf[...] = jnp.zeros((128, ROWS), F32)
 
     @pl.loop(0, 4)
-    def _(i):
-        g = lax.rem(group + 1 + i, 4)
+    def _(back):
+        i = 3 - back
+        dz = i + i // 2 - 2 * (i // 3)
 
         def put(b, dk, dv):
-            dst = g * 4 + b
-            gkv_s[dst, 0] = dk.astype(BF16)
-            gkv_s[dst, 1] = dv.astype(BF16)
-
-            @pl.when(dst != seq)
+            slot = in_seq(b // 2, dz, b % 2)
+            gkv_s[slot, 0] = dk.astype(BF16)
+            gkv_s[slot, 1] = dv.astype(BF16)
+
+            @pl.when(core != b % 2)
             def _():
-                grad_copy(seq, dst).start()
+                gx_copy(slot).start()
 
         dq = backward(
-            lambda b: kv[g * 4 + b, 0],
-            lambda b: kv[g * 4 + b, 1],
+            lambda b: kv[in_seq(b // 2, dz, b % 2), 0],
+            lambda b: kv[in_seq(b // 2, dz, b % 2), 1],
             lambda h: gf_t[h],
             lambda h: gf_n[h],
             lambda h: qf_n[h],
-            lambda h: e_far.at[h, g],
-            lambda h: fac_f[h, g],
+            lambda h: e_far.at[h, i],
+            lambda h: fac_f[h, i],
             lambda h: delta_f[h],
             put,
         )
@@ -432,28 +522,50 @@
             half = slice(h * HALF, (h + 1) * HALF)
             acc_qf[half] = acc_qf[half] + dq[h]
 
-    @pl.loop(1, NSEQ)
-    def _(i):
-        dw_copy(peer_s(i), i).wait_recv()
-
-    part = dwr[0]
-    for j in range(1, NSEQ):
-        part = part + dwr[j]
-    dws[...] = part
-    dwf[seq] = part
-
-    def df_copy(slot, i):
-        return remote(dws, dwf.at[slot], df_send.at[i], df_recv.at[slot], "seq", peer_s(i))
-
-    @pl.loop(1, NSEQ)
-    def _(i):
-        df_copy(seq, i).start()
+        @pl.when(back > 0)
+        def _():
+            merge(i + 1)
+
+        @pl.when(back == 0)
+        def _():
+            dx_copy(core).wait_recv()
+            dwm[...] = dwp[core] + dwx[...]
+            for n in range(1, 8):
+                dw_copy(chip, n).start()
+
+        @pl.when(back == 3)
+        def _():
+            for n in range(1, 8):
+                dw_copy(peer_c(n), n).wait_recv()
+            dwr[chip] = dwm[chip]
+            part = dwr[0]
+            for n in range(1, 8):
+                part = part + dwr[n]
+            dwf[core, chip] = part.astype(BF16)
+            for n in range(1, 8):
+                df_copy(chip, n).start()
 
     acc_k[...] = jnp.zeros((4, ROWS, 128), F32)
     acc_v[...] = jnp.zeros((4, ROWS, 128), F32)
 
     @pl.loop(0, RATE)
     def _(r):
+        @pl.when(r == 1)
+        def _():
+            merge(0)
+
+        @pl.when(r == 2)
+        def _():
+            for n in range(1, 8):
+                w_copy(peer_h(n), n).wait_recv()
+                w_share(peer_h(n), core).start()
+
+        @pl.when(r == 3)
+        def _():
+            for n in range(1, 8):
+                df_copy(peer_c(n), n).wait_recv()
+            dc_copy(core).start()
+
         def put(b, dk, dv):
             acc_k[b] = acc_k[b] + dk
             acc_v[b] = acc_v[b] + dv
@@ -480,7 +592,7 @@
 
     @pl.loop(1, NHEAD)
     def _(i):
-        w_copy(peer_h(i), i).wait_recv()
+        w_share(peer_h(i), 1 - core).wait_recv()
         at_copy(peer_h(i), i).wait_recv()
 
     from_rm = jnp.where(rm_row == lax.rem(rm_col, 32) * RATE + rm_col // 32, 1.0, 0.0).astype(BF16)
@@ -490,14 +602,14 @@
         result = result + nn(rows, ws[h])
     lo_ref[...] = result.astype(BF16)
 
-    @pl.loop(1, NSEQ)
-    def _(i):
-        grad_copy(peer_s(i), peer_s(i)).wait_recv()
-
-    gkv_r[seq] = gkv_s[seq]
+    @pl.loop(1, 8)
+    def _(i):
+        grad_copy(seq, peer_c(i), partner).wait_recv()
+
+    gkv_r[chip] = gkv_s[seq]
     sum_k = gkv_r[0, 0].astype(F32)
     sum_v = gkv_r[0, 1].astype(F32)
-    for j in range(1, NSEQ):
+    for j in range(1, 8):
         sum_k = sum_k + gkv_r[j, 0].astype(F32)
         sum_v = sum_v + gkv_r[j, 1].astype(F32)
     dk_parts = []
@@ -509,26 +621,35 @@
     dk_ref[...] = nn(jnp.concatenate(dk_parts, axis=1), perm[...]).astype(BF16)
     dv_ref[...] = nn(jnp.concatenate(dv_parts, axis=1), perm[...]).astype(BF16)
 
-    @pl.loop(1, NSEQ)
-    def _(i):
-        df_copy(peer_s(i), i).wait_recv()
-
-    whole = dwf[...].reshape(128, WIDTH)
-    dw_ref[0:48] = whole[0:48].astype(BF16)
-    dw_ref[48:96] = whole[64:112].astype(BF16)
-
-    @pl.loop(1, NSEQ)
-    def _(i):
-        kv_copy(seq, i).wait_send()
-        dw_copy(seq, i).wait_send()
-        df_copy(seq, i).wait_send()
-        grad_copy(seq, peer_s(i)).wait_send()
-
-    @pl.loop(1, NHEAD)
-    def _(i):
-        dy_copy(head, i).wait_send()
+    dc_copy(1 - core).wait_recv()
+    for half in range(2):
+        whole = dwf[half].reshape(128, 384)
+        dw_ref[0:48, half * 384 : (half + 1) * 384] = whole[0:48]
+        dw_ref[48:96, half * 384 : (half + 1) * 384] = whole[64:112]
+
+    dx_copy(1 - core).wait_send()
+    dc_copy(core).wait_send()
+
+    @pl.loop(0, 15)
+    def _(i):
+        kv_copy(seq, i, partner).wait_send()
+
+    @pl.loop(0, 7)
+    def _(i):
+        dy_copy(head, i, partner_h).wait_send()
+
+    @pl.loop(1, 8)
+    def _(i):
         w_copy(head, i).wait_send()
+        w_share(peer_h(i), core).wait_send()
         at_copy(head, i).wait_send()
+        dw_copy(chip, i).wait_send()
+        df_copy(chip, i).wait_send()
+        grad_copy(at_chip(peer_c(i)), chip, partner).wait_send()
+
+    @pl.loop(0, 8)
+    def _(i):
+        gx_copy(i * 2 + 1 - core).wait_send()
 
 
 def body(queries, keys, values, slide_ids, head_shift_list, out_weight, d_y):
@@ -576,12 +697,14 @@
             pltpu.VMEM((NHEAD, RATE, 32, 128), BF16),
             pltpu.VMEM((RATE, ROWS, WIDTH), BF16),
             pltpu.VMEM((NHEAD, 128, WIDTH), BF16),
-            pltpu.VMEM((NSEQ, 8, WIDTH), F32),
-            pltpu.VMEM((NSEQ, 8, WIDTH), F32),
-            pltpu.VMEM((8, WIDTH), F32),
-            pltpu.VMEM((NSEQ, 8, WIDTH), F32),
+            pltpu.VMEM((2, 8, 16, 384), F32),
+            pltpu.VMEM((8, 16, 384), F32),
+            pltpu.VMEM((8, 16, 384), F32),
+            pltpu.VMEM((8, 16, 384), F32),
+            pltpu.VMEM((2, 8, 16, 384), BF16),
             pltpu.VMEM((NSEQ, 2, ROWS, 128), BF16),
             pltpu.VMEM((NSEQ, 2, ROWS, 128), BF16),
+            pltpu.VMEM((8, 2, ROWS, 128), BF16),
             pltpu.VMEM((4, ROWS, 128), F32),
             pltpu.VMEM((4, ROWS, 128), F32),
             pltpu.VMEM((RATE, 128, ROWS), F32),
@@ -594,12 +717,18 @@
             sems((NHEAD,)),
             sems((NHEAD,)),
             sems((NHEAD,)),
+            sems((NHEAD,)),
+            sems((NHEAD,)),
+            sems((2,)),
+            sems((8,)),
+            sems((8,)),
+            sems((8,)),
+            sems((8,)),
+            sems((2,)),
             sems((NSEQ,)),
             sems((NSEQ,)),
-            sems((NSEQ,)),
-            sems((NSEQ,)),
-            sems((NSEQ,)),
-            sems((NSEQ,)),
+            sems((8,)),
+            sems((8,)),
         ],
         compiler_params=pltpu.CompilerParams(
             collective_id=0, has_side_effects=True, vmem_limit_bytes=56 * 1024 * 1024

time: 124 us -> 69.2 us (0.56)
  the two profiles are of different devices: /device:TPU:125 before, /device:TPU:1 now
where the time goes in v1:
time: 69.2 us; the launch traced here: 69 us
  Pallas kernels  63.1 us (91%)
  local copies, waits for them, and re-layouts  5.29 us (8%)
    pallas_call x1, Pallas kernels, body(): pl.pallas_call(kernel, out_shape=(jax.ShapeDtypeStruct((128, WIDTH), BF16...  63.1 us
    unnamed x13, local copies, waits for them, and re-layouts  5.29 us

profile of v1, /device:TPU:1, one launch (start us, length us, event | category | flops | bytes accessed | tf_op | source)
XLA Modules:
  0.0 69.0 jit_solution(15584171014039296745)
XLA Ops:
  0.6 63.1 %shard_map.110 = (bf16[128,768]{1,0:T(8,128)(2,1)}, bf16[256,384]{1,0:T(8,128)(2,1)}, bf16[256,384]{1,0:T(8,128)(2,1)}, bf16[256,384]{1,0:T(8,128)(2,1)}, bf16[96,768]{1,0:T(8,128)(2,1)}) custom-call(bf16[256,384]{1,0:T(8,128)(2,1)} %q_ref.1, bf16[256,384]{1,0:T(8,128)(2,1)} %k_ref.1, bf16[256,384]{1,0:T(8,128)(2,1)} %v_ref.1, s32[8,128]{1,0:T(8,128)} %bitcast.1, ...), custom_call_target="tpu_custom_call" | custom-call | flops 3000000000 | bytes 4000000 | tf_op jit(solution)/shard_map/pallas_call | solution.py:659
  63.7 0.0 copy-start.2
  63.7 1.7 %copy.17 = bf16[128,768]{1,0:T(8,128)(2,1)} copy(bf16[128,768]{1,0:T(8,128)(2,1)} %get-tuple-element.10) | data formatting | bytes 393216
  65.4 0.0 copy-done.2
  65.4 0.0 copy-start.1
  65.4 0.7 copy.18
  66.1 0.3 copy-done.1
  66.4 0.0 copy-start
  66.4 0.7 copy.19
  67.0 0.3 copy-done
  67.4 0.0 copy-start.3
  67.4 0.7 copy.20
  68.0 0.3 copy-done.3
  68.3 0.7 copy.21
Async XLA Ops:
  63.7 1.7 %copy-start.2 = (bf16[256,384]{1,0:T(8,128)(2,1)S(1)}, bf16[256,384]{1,0:T(8,128)(2,1)}, u32[]{:S(2)}) copy-start(bf16[256,384]{1,0:T(8,128)(2,1)} %get-tuple-element.11) | copy-start | bytes 589828
  65.4 1.0 %copy-start.1 = (bf16[256,384]{1,0:T(8,128)(2,1)S(1)}, bf16[256,384]{1,0:T(8,128)(2,1)}, u32[]{:S(2)}) copy-start(bf16[256,384]{1,0:T(8,128)(2,1)} %get-tuple-element.12) | copy-start | bytes 589828
  66.4 1.0 %copy-start = (bf16[256,384]{1,0:T(8,128)(2,1)S(1)}, bf16[256,384]{1,0:T(8,128)(2,1)}, u32[]{:S(2)}) copy-start(bf16[256,384]{1,0:T(8,128)(2,1)} %get-tuple-element.13) | copy-start | bytes 589828
  67.4 1.0 %copy-start.3 = (bf16[96,768]{1,0:T(8,128)(2,1)S(1)}, bf16[96,768]{1,0:T(8,128)(2,1)}, u32[]{:S(2)}) copy-start(bf16[96,768]{1,0:T(8,128)(2,1)} %get-tuple-element.14) | copy-start | bytes 442372

commit v2 on v1

v2 whole, which is shorter than its diff:
```python
import math

import jax
import jax.numpy as jnp
from jax import lax
from jax.experimental import pallas as pl
from jax.experimental.pallas import tpu as pltpu
from jax.sharding import PartitionSpec as P

HEAD = 48
HALF = 64
RATE = 4
ROWS = 256
WIDTH = 768
NSEQ = 16
NHEAD = 8
SAME = 8192.0
SCALE = 1.0 / math.sqrt(HEAD)
EXP2 = SCALE * math.log2(math.e)
F32 = jnp.float32
BF16 = jnp.bfloat16


def nt(a, b):
    return lax.dot_general(a, b, (((1,), (1,)), ((), ())), preferred_element_type=F32)


def nn(a, b):
    return jnp.dot(a, b, preferred_element_type=F32)


def iota(shape, dim):
    return lax.broadcasted_iota(jnp.int32, shape, dim)


def remote(src, dst, send, recv, axis, index):
    return pltpu.make_async_remote_copy(
        src_ref=src,
        dst_ref=dst,
        send_sem=send,
        recv_sem=recv,
        device_id={axis: index},
        device_id_type=pl.DeviceIdType.MESH,
    )


def kernel(
    q_ref,
    k_ref,
    v_ref,
    id_ref,
    shift_ref,
    w_ref,
    dy_ref,
    lo_ref,
    dq_ref,
    dk_ref,
    dv_ref,
    dw_ref,
    perm,
    near_k,
    near_v,
    kv,
    q_t,
    q_n,
    g_t,
    g_n,
    e_near,
    e_far,
    top_n,
    sum_n,
    out_n,
    top_f,
    sum_f,
    out_f,
    fac_n,
    fac_f,
    delta,
    attn_t,
    attn_n,
    attn_r,
    dys,
    ws,
    dwp,
    dwx,
    dwm,
    dwr,
    dwf,
    gkv_s,
    gkv_x,
    gkv_r,
    gkv_p,
    gkv_y,
    acc_k,
    acc_v,
    acc_q,
    kv_send,
    kv_recv,
    dy_send,
    dy_recv,
    w_send,
    w_recv,
    ws_send,
    ws_recv,
    at_send,
    at_recv,
    dx_sem,
    dw_send,
    dw_recv,
    df_send,
    df_recv,
    dc_sem,
    gx_send,
    gx_recv,
    g_send,
    g_recv,
    gy_sem,
):
    seq = lax.axis_index("seq")
    head = lax.axis_index("head")

    x_lo, z, core = seq // 8, lax.rem(seq // 2, 4), lax.rem(seq, 2)
    x_hi, y = head // 4, lax.rem(head, 4)
    chip = seq // 2

    def at_chip(j):
        return j * 2 + core

    def in_seq(x, dz, c):
        return x * 8 + lax.rem(z + dz, 4) * 2 + c

    def in_head(x, dy):
        return x * 4 + lax.rem(y + dy, 4)

    def peer_c(i):
        return lax.rem(chip + i, 8)

    def peer_h(i):
        return lax.rem(head + i, NHEAD)

    sibling = in_seq(x_lo, 0, 1 - core)
    partner = in_seq(1 - x_lo, 0, core)
    partner_h = in_head(1 - x_hi, 0)
    turns = (1, 3, 2)

    barrier = pltpu.get_barrier_semaphore()
    pl.semaphore_signal(
        barrier, inc=1, device_id={"seq": sibling}, device_id_type=pl.DeviceIdType.MESH
    )

    @pl.loop(1, 8)
    def _(i):
        pl.semaphore_signal(
            barrier,
            inc=1,
            device_id={"seq": at_chip(peer_c(i))},
            device_id_type=pl.DeviceIdType.MESH,
        )
        pl.semaphore_signal(
            barrier, inc=1, device_id={"head": peer_h(i)}, device_id_type=pl.DeviceIdType.MESH
        )

    slide_col = lax.rem(iota((128, 128), 0), HALF) - HEAD
    below = jnp.zeros((128, 128), F32)
    upto = jnp.zeros((128, 128), F32)
    for s in range(8):
        ids = id_ref[s : s + 1, :]
        below = below + jnp.where(ids < slide_col, 1.0, 0.0)
        upto = upto + jnp.where(ids <= slide_col, 1.0, 0.0)
    ones = jnp.ones((8, 128), BF16)
    first_row = nt(ones, below.astype(BF16))[0:1, :]
    last_row = nt(ones, upto.astype(BF16))[0:1, :]
    first_col = jnp.sum(below, axis=1, keepdims=True)
    last_col = jnp.sum(upto, axis=1, keepdims=True)

    shift0 = shift_ref[2 * head]
    shift1 = shift_ref[2 * head + 1]
    lane_row = iota((1, 128), 1)
    lane_col = iota((128, 1), 0)
    shift_row = jnp.where(lane_row < HALF, shift0, shift1)
    shift_col = jnp.where(lane_col < HALF, shift0, shift1)
    hot_row = lax.rem(lane_row, HALF) >= HEAD
    hot_col = lax.rem(lane_col, HALF) >= HEAD

    def turned(shift, j):
        return jnp.bitwise_and(shift + 1 + j, RATE - 1)

    def to_slot(parts, shift, j):
        out = parts[0]
        for r in range(1, RATE):
            out = jnp.where(turned(shift, j) == r, parts[r], out)
        return out

    def from_slot(parts, shift, r):
        out = parts[0]
        for j in range(1, RATE):
            out = jnp.where(turned(shift, j) == r, parts[j], out)
        return out

    within = lax.rem(lane_col, HALF)
    source = (lane_col // HALF) * (RATE * HEAD) + within
    given = iota((128, 384), 1)
    for r in range(RATE):
        held = jnp.where(within < HEAD, source + r * HEAD, -1)
        perm[r * 128 : (r + 1) * 128] = jnp.where(given == held, 1.0, 0.0).astype(BF16)
    k_p = nt(k_ref[...], perm[...])
    v_p = nt(v_ref[...], perm[...])
    far_k = jnp.zeros((ROWS, 128), F32)
    far_v = jnp.zeros((ROWS, 128), F32)
    for r in range(RATE):
        at = (iota((ROWS, 128), 0) * RATE + r).astype(F32)
        hot = jnp.where(hot_row & (at >= first_row) & (at < last_row), 1.0, 0.0)
        k_r = k_p[:, r * 128 : (r + 1) * 128] + hot
        v_r = v_p[:, r * 128 : (r + 1) * 128]
        near_k[r] = k_r.astype(BF16)
        near_v[r] = v_r.astype(BF16)
        far_k = jnp.where(shift_row == r, k_r, far_k)
        far_v = jnp.where(shift_row == r, v_r, far_v)
    kv[seq, 0] = far_k.astype(BF16)
    kv[seq, 1] = far_v.astype(BF16)

    rm_row = iota((128, 128), 0)
    rm_col = iota((128, 128), 1)
    to_rm = jnp.where(rm_col == lax.rem(rm_row, 32) * RATE + rm_row // 32, 1.0, 0.0).astype(BF16)
    dy_own = nn(to_rm, dy_ref[...]).astype(BF16)
    own_rows = pl.ds(pl.multiple_of(head * 32, 32), 32)
    for r in range(RATE):
        dys[r, own_rows, :] = dy_own[r * 32 : (r + 1) * 32]

    zeros16 = jnp.zeros((16, WIDTH), BF16)
    ws[head, 0:48] = w_ref[0:48]
    ws[head, 64:112] = w_ref[48:96]
    for h in range(NHEAD):
        ws[h, 48:64] = zeros16
        ws[h, 112:128] = zeros16

    pl.semaphore_wait(barrier, 15)

    def kv_copy(slot, i, dst):
        return remote(kv.at[slot], kv.at[slot], kv_send.at[i], kv_recv.at[slot], "seq", dst)

    def dy_copy(owner, i, dst):
        rows = pl.ds(pl.multiple_of(owner * 32, 32), 32)
        part = dys.at[:, rows, :]
        return remote(part, part, dy_send.at[i], dy_recv.at[owner], "head", dst)

    def w_copy(owner, i):
        part = ws.at[owner, pl.ds(pl.multiple_of(core * HALF, HALF), HEAD)]
        return remote(part, part, w_send.at[i], w_recv.at[owner], "head", peer_h(i))

    def w_share(owner, half):
        part = ws.at[owner, pl.ds(pl.multiple_of(half * HALF, HALF), HEAD)]
        return remote(part, part, ws_send.at[owner], ws_recv.at[owner], "seq", sibling)

    kv_copy(seq, 0, partner).start()
    for j, turn in enumerate(turns):
        kv_copy(seq, 1 + j, in_seq(x_lo, turn, core)).start()
    kv_copy(seq, 4, sibling).start()
    dy_copy(head, 0, partner_h).start()
    for n, turn in enumerate(turns):
        dy_copy(head, 1 + n, in_head(x_hi, turn)).start()

    q_p = nt(q_ref[...], perm[...])
    q_pt = nt(perm[...], q_ref[...])
    q_rows = []
    q_cols = []
    for r in range(RATE):
        at = (iota((128, ROWS), 1) * RATE + r).astype(F32)
        hot = jnp.where(hot_col & (at >= first_col) & (at < last_col), SAME, 0.0)
        q_rows.append(q_p[:, r * 128 : (r + 1) * 128])
        q_cols.append(q_pt[r * 128 : (r + 1) * 128, :] + hot)
    for j in range(RATE):
        q_j = to_slot(q_rows, shift_row, j)
        q_jt = to_slot(q_cols, shift_col, j)
        q_n[0, j] = jnp.where(lane_row < HALF, q_j, 0.0).astype(BF16)
        q_n[1, j] = jnp.where(lane_row < HALF, 0.0, q_j).astype(BF16)
        q_t[0, j] = jnp.where(lane_col < HALF, q_jt, 0.0).astype(BF16)
        q_t[1, j] = jnp.where(lane_col < HALF, 0.0, q_jt).astype(BF16)

    def forward(keys, vals, q_of, e_of, h):
        top = None
        for b in range(4):
            s = nn(keys(b), q_of)
            e_of[b] = s
            m = jnp.max(s, axis=0, keepdims=True)
            top = m if top is None else jnp.maximum(top, m)
        total = jnp.zeros((1, ROWS), F32)
        out = jnp.zeros((HALF, ROWS), F32)
        for b in range(4):
            e = jnp.exp2((e_of[b] - top) * EXP2)
            e_of[b] = e
            total = total + jnp.sum(e, axis=0, keepdims=True)
            v_t = vals(b).T[h * HALF : (h + 1) * HALF]
            out = out + nn(v_t, e.astype(BF16))
        return top, total, out

    halves = (slice(0, HALF), slice(HALF, 2 * HALF))

    @pl.loop(0, RATE)
    def _(j):
        for h in range(2):
            top, total, out = forward(
                lambda b: near_k[b], lambda b: near_v[b], q_t[h, j], e_near.at[h, j], h
            )
            top_n[h] = top
            sum_n[h] = total
            out_n[h] = out
            inverse = 1.0 / total
            fac_n[h, j] = inverse
            attn_t[j, halves[h]] = (out * inverse).astype(BF16)

        @pl.when(j == 0)
        def _():
            kv_copy(partner, 0, partner).wait_recv()
            for n, turn in enumerate(turns):
                kv_copy(partner, 5 + n, in_seq(x_lo, turn, core)).start()
            kv_copy(partner, 8, sibling).start()

        @pl.when(j == 1)
        def _():
            dy_copy(partner_h, 0, partner_h).wait_recv()
            for n, turn in enumerate(turns):
                dy_copy(partner_h, 4 + n, in_head(x_hi, turn)).start()

    def share(i):
        dz = i + i // 2 - 2 * (i // 3)
        for x in range(2):
            slot = in_seq(x, dz, core)
            kv_copy(slot, 0, partner).wait_recv()
            kv_copy(slot, 9 + 2 * (i - 1) + x, sibling).start()

    def far_forward(i):
        dz = i + i // 2 - 2 * (i // 3)
        for x in range(2):
            kv_copy(in_seq(x, dz, 1 - core), 0, partner).wait_recv()
        for h in range(2):
            top, total, out = forward(
                lambda b: kv[in_seq(b // 2, dz, b % 2), 0],
                lambda b: kv[in_seq(b // 2, dz, b % 2), 1],
                q_t[h, 3],
                e_far.at[h, i],
                h,
            )
            top_f[h, i] = top
            sum_f[h, i] = total
            out_f[h, i] = out

    @pl.loop(0, 4)
    def _(i):
        @pl.when(i == 1)
        def _():
            share(1)

        @pl.when((i == 1) | (i == 2))
        def _():
            share(i + 1)

        far_forward(i)

    for h in range(2):
        top = top_n[h]
        for i in range(4):
            top = jnp.maximum(top, top_f[h, i])
        weight = jnp.exp2((top_n[h] - top) * EXP2)
        total = weight * sum_n[h]
        out = weight * out_n[h]
        weights = []
        for i in range(4):
            w_i = jnp.exp2((top_f[h, i] - top) * EXP2)
            weights.append(w_i)
            total = total + w_i * sum_f[h, i]
            out = out + w_i * out_f[h, i]
        inverse = 1.0 / total
        fac_n[h, 3] = weight * inverse
        for i in range(4):
            fac_f[h, i] = weights[i] * inverse
        attn_t[3, halves[h]] = (out * inverse).astype(BF16)

    attn_slots = [attn_t[j].astype(F32) for j in range(RATE)]
    attn_rt = [from_slot(attn_slots, shift_col, r) for r in range(RATE)]
    for r in range(RATE):
        attn_n[r] = attn_rt[r].T.astype(BF16)

    def at_copy(slot, i):
        rows = pl.ds(pl.multiple_of(peer_h(i) * 32, 32), 32)
        return remote(
            attn_n.at[:, rows, :], attn_r.at[slot], at_send.at[i], at_recv.at[slot], "head", peer_h(i)
        )

    for n in range(1, NHEAD):
        at_copy(head, n).start()
    for r in range(RATE):
        attn_r[head, r] = attn_n[r, own_rows, :]

    for turn in turns:
        for x in range(2):
            dy_copy(in_head(x, turn), 0, partner_h).wait_recv()
    for n in range(1, NHEAD):
        w_copy(head, n).start()

    w_own = ws[head]
    g_rows = []
    g_cols = []
    weight_grad = jnp.zeros((128, WIDTH), F32)
    for r in range(RATE):
        g_rows.append(nt(dys[r], w_own))
        g_cols.append(nt(w_own, dys[r]))
        weight_grad = weight_grad + nn(attn_rt[r].astype(BF16), dys[r])
    for j in range(RATE):
        g_j = to_slot(g_rows, shift_row, j)
        g_jt = to_slot(g_cols, shift_col, j)
        g_n[0, j] = jnp.where(lane_row < HALF, g_j, 0.0).astype(BF16)
        g_n[1, j] = jnp.where(lane_row < HALF, 0.0, g_j).astype(BF16)
        g_t[0, j] = jnp.where(lane_col < HALF, g_jt, 0.0).astype(BF16)
        g_t[1, j] = jnp.where(lane_col < HALF, 0.0, g_jt).astype(BF16)
        for h in range(2):
            product = g_t[h, j, halves[h], :].astype(F32) * attn_t[j, halves[h]].astype(F32)
            delta[h, j] = jnp.sum(product, axis=0, keepdims=True)

    for half in range(2):
        for n in range(8):
            dwp[half, n] = weight_grad[n * 16 : (n + 1) * 16, half * 384 : (half + 1) * 384]

    def dx_copy(half):
        return remote(dwp.at[half], dwx, dx_sem.at[0], dx_sem.at[1], "seq", sibling)

    def dw_copy(sender, i):
        dst = peer_c(i)
        return remote(dwm.at[dst], dwr.at[sender], dw_send.at[i], dw_recv.at[sender], "seq", at_chip(dst))

    def df_copy(sender, i):
        part = dwf.at[core, sender]
        return remote(part, part, df_send.at[i], df_recv.at[sender], "seq", at_chip(peer_c(i)))

    def dc_copy(half):
        return remote(dwf.at[half], dwf.at[half], dc_sem.at[0], dc_sem.at[1], "seq", sibling)

    dx_copy(1 - core).start()

    def weight_over_cores():
        dx_copy(core).wait_recv()
        dwm[...] = dwp[core] + dwx[...]
        for n in range(1, 8):
            dw_copy(chip, n).start()

    def weight_over_chips():
        for n in range(1, 8):
            dw_copy(peer_c(n), n).wait_recv()
        dwr[chip] = dwm[chip]
        part = dwr[0]
        for n in range(1, 8):
            part = part + dwr[n]
        dwf[core, chip] = part.astype(BF16)
        for n in range(1, 8):
            df_copy(chip, n).start()

    def weight_to_sibling():
        for n in range(1, 8):
            df_copy(peer_c(n), n).wait_recv()
        dc_copy(core).start()

    def backward(keys, vals, j, e_of, factor, put):
        dq = [jnp.zeros((HALF, ROWS), F32), jnp.zeros((HALF, ROWS), F32)]
        for b in range(4):
            k_t = keys(b).T
            val = vals(b)
            dk = jnp.zeros((ROWS, 128), F32)
            dv = jnp.zeros((ROWS, 128), F32)
            for h in range(2):
                p = e_of(h)[b] * factor(h)
                ds = (p * (nn(val, g_t[h, j]) - delta[h, j])).astype(BF16)
                dv = dv + nn(p.astype(BF16), g_n[h, j])
                dk = dk + nn(ds, q_n[h, j])
                dq[h] = dq[h] + nn(k_t[halves[h]], ds)
            put(b, dk, dv)
        return dq

    acc_k[...] = jnp.zeros((4, ROWS, 128), F32)
    acc_v[...] = jnp.zeros((4, ROWS, 128), F32)

    def near_backward(j):
        def put(b, dk, dv):
            acc_k[b] = acc_k[b] + dk
            acc_v[b] = acc_v[b] + dv

        dq = backward(
            lambda b: near_k[b],
            lambda b: near_v[b],
            j,
            lambda h: e_near.at[h, j],
            lambda h: fac_n[h, j],
            put,
        )
        for h in range(2):
            acc_q[j, halves[h]] = dq[h]

    def gx_copy(slot):
        return remote(
            gkv_s.at[slot], gkv_x.at[slot], gx_send.at[slot], gx_recv.at[slot], "seq", sibling
        )

    def grad_copy(x, dz):
        slot = in_seq(x, dz, core)
        index = dz + 4 * (x != x_lo)
        return remote(
            gkv_s.at[slot],
            gkv_r.at[index],
            g_send.at[index],
            g_recv.at[index],
            "seq",
            in_seq(x_lo, dz, core),
        )

    def gy_copy():
        return remote(gkv_p, gkv_y, gy_sem.at[0], gy_sem.at[1], "seq", partner)

    def merge(i):
        dz = i + i // 2 - 2 * (i // 3)
        for x in range(2):
            slot = in_seq(x, dz, core)
            gx_copy(slot).wait_recv()
            for n in range(2):
                gkv_s[slot, n] = (
                    gkv_s[slot, n].astype(F32) + gkv_x[slot, n].astype(F32)
                ).astype(BF16)

            @pl.when(dz != 0)
            def _():
                grad_copy(x, dz).start()

    def sum_partner():
        for turn in turns:
            grad_copy(1 - x_lo, turn).wait_recv()
        for n in range(2):
            total = gkv_s[partner, n].astype(F32)
            for turn in turns:
                total = total + gkv_r[4 + turn, n].astype(F32)
            gkv_p[n] = total.astype(BF16)
        gy_copy().start()

    acc_q[3] = jnp.zeros((128, ROWS), F32)

    @pl.loop(0, 4)
    def _(back):
        i = 3 - back
        dz = i + i // 2 - 2 * (i // 3)

        def put(b, dk, dv):
            slot = in_seq(b // 2, dz, b % 2)
            gkv_s[slot, 0] = dk.astype(BF16)
            gkv_s[slot, 1] = dv.astype(BF16)

            @pl.when(core != b % 2)
            def _():
                gx_copy(slot).start()

        dq = backward(
            lambda b: kv[in_seq(b // 2, dz, b % 2), 0],
            lambda b: kv[in_seq(b // 2, dz, b % 2), 1],
            3,
            lambda h: e_far.at[h, i],
            lambda h: fac_f[h, i],
            put,
        )
        for h in range(2):
            acc_q[3, halves[h]] = acc_q[3, halves[h]] + dq[h]

        @pl.when(back > 0)
        def _():
            merge(i + 1)

        @pl.when(back == 0)
        def _():
            weight_over_cores()

        @pl.when(back == 3)
        def _():
            weight_over_chips()

    acc_far = acc_q[3]
    merge(0)

    @pl.loop(0, RATE)
    def _(j):
        near_backward(j)

        @pl.when(j == 1)
        def _():
            weight_to_sibling()
            for n in range(1, NHEAD):
                w_copy(peer_h(n), n).wait_recv()
                w_share(peer_h(n), core).start()

        @pl.when(j == 2)
        def _():
            sum_partner()

    acc_q[3] = acc_q[3] + acc_far
    dq_slots = [(acc_q[j] * SCALE).T for j in range(RATE)]
    dq_parts = [from_slot(dq_slots, shift_row, r).astype(BF16) for r in range(RATE)]
    dq_ref[...] = nn(jnp.concatenate(dq_parts, axis=1), perm[...]).astype(BF16)

    for n in range(1, NHEAD):
        w_share(peer_h(n), 1 - core).wait_recv()
        at_copy(peer_h(n), n).wait_recv()
    from_rm = jnp.where(rm_row == lax.rem(rm_col, 32) * RATE + rm_col // 32, 1.0, 0.0).astype(BF16)
    result = jnp.zeros((128, WIDTH), F32)
    for h in range(NHEAD):
        rows = nn(from_rm, attn_r[h].reshape(128, 128)).astype(BF16)
        result = result + nn(rows, ws[h])
    lo_ref[...] = result.astype(BF16)

    for turn in turns:
        grad_copy(x_lo, turn).wait_recv()
    gy_copy().wait_recv()
    far = []
    for n in range(2):
        total = gkv_s[seq, n].astype(F32) + gkv_y[n].astype(F32)
        for turn in turns:
            total = total + gkv_r[turn, n].astype(F32)
        far.append(total)
    sum_k, sum_v = far
    dk_parts = []
    dv_parts = []
    for r in range(RATE):
        mine = shift_row == r
        dk_parts.append(((acc_k[r] + jnp.where(mine, sum_k, 0.0)) * SCALE).astype(BF16))
        dv_parts.append((acc_v[r] + jnp.where(mine, sum_v, 0.0)).astype(BF16))
    dk_ref[...] = nn(jnp.concatenate(dk_parts, axis=1), perm[...]).astype(BF16)
    dv_ref[...] = nn(jnp.concatenate(dv_parts, axis=1), perm[...]).astype(BF16)

    dc_copy(1 - core).wait_recv()
    for half in range(2):
        whole = dwf[half].reshape(128, 384)
        dw_ref[0:48, half * 384 : (half + 1) * 384] = whole[0:48]
        dw_ref[48:96, half * 384 : (half + 1) * 384] = whole[64:112]

    dx_copy(1 - core).wait_send()
    dc_copy(core).wait_send()

    @pl.loop(0, 15)
    def _(i):
        kv_copy(seq, i, partner).wait_send()

    @pl.loop(1, 8)
    def _(i):
        w_copy(head, i).wait_send()
        w_share(peer_h(i), core).wait_send()
        dy_copy(head, i - 1, partner_h).wait_send()
        at_copy(head, i).wait_send()
        dw_copy(chip, i).wait_send()
        df_copy(chip, i).wait_send()

    @pl.loop(0, 8)
    def _(i):
        gx_copy(i * 2 + 1 - core).wait_send()

    gy_copy().wait_send()
    for turn in turns:
        for x in range(2):
            grad_copy(x, turn).wait_send()


def finish(*refs):
    for source, target in zip(refs[:5], refs[5:], strict=True):
        target[...] = source[...]


def body(queries, keys, values, slide_ids, head_shift_list, out_weight, d_y):
    vmem = pl.BlockSpec(memory_space=pltpu.VMEM)
    smem = pl.BlockSpec(memory_space=pltpu.SMEM)
    sems = pltpu.SemaphoreType.DMA
    results = pl.pallas_call(
        kernel,
        out_shape=(
            jax.ShapeDtypeStruct((128, WIDTH), BF16),
            jax.ShapeDtypeStruct((ROWS, 384), BF16),
            jax.ShapeDtypeStruct((ROWS, 384), BF16),
            jax.ShapeDtypeStruct((ROWS, 384), BF16),
            jax.ShapeDtypeStruct((96, WIDTH), BF16),
        ),
        in_specs=[vmem, vmem, vmem, vmem, smem, vmem, vmem],
        out_specs=(vmem,) * 5,
        scratch_shapes=[
            pltpu.VMEM((4 * 128, 384), BF16),
            pltpu.VMEM((4, ROWS, 128), BF16),
            pltpu.VMEM((4, ROWS, 128), BF16),
            pltpu.VMEM((NSEQ, 2, ROWS, 128), BF16),
            pltpu.VMEM((2, RATE, 128, ROWS), BF16),
            pltpu.VMEM((2, RATE, ROWS, 128), BF16),
            pltpu.VMEM((2, RATE, 128, ROWS), BF16),
            pltpu.VMEM((2, RATE, ROWS, 128), BF16),
            pltpu.VMEM((2, RATE, 4, ROWS, ROWS), F32),
            pltpu.VMEM((2, 4, 4, ROWS, ROWS), F32),
            pltpu.VMEM((2, 1, ROWS), F32),
            pltpu.VMEM((2, 1, ROWS), F32),
            pltpu.VMEM((2, HALF, ROWS), F32),
            pltpu.VMEM((2, 4, 1, ROWS), F32),
            pltpu.VMEM((2, 4, 1, ROWS), F32),
            pltpu.VMEM((2, 4, HALF, ROWS), F32),
            pltpu.VMEM((2, RATE, 1, ROWS), F32),
            pltpu.VMEM((2, 4, 1, ROWS), F32),
            pltpu.VMEM((2, RATE, 1, ROWS), F32),
            pltpu.VMEM((RATE, 128, ROWS), BF16),
            pltpu.VMEM((RATE, ROWS, 128), BF16),
            pltpu.VMEM((NHEAD, RATE, 32, 128), BF16),
            pltpu.VMEM((RATE, ROWS, WIDTH), BF16),
            pltpu.VMEM((NHEAD, 128, WIDTH), BF16),
            pltpu.VMEM((2, 8, 16, 384), F32),
            pltpu.VMEM((8, 16, 384), F32),
            pltpu.VMEM((8, 16, 384), F32),
            pltpu.VMEM((8, 16, 384), F32),
            pltpu.VMEM((2, 8, 16, 384), BF16),
            pltpu.VMEM((NSEQ, 2, ROWS, 128), BF16),
            pltpu.VMEM((NSEQ, 2, ROWS, 128), BF16),
            pltpu.VMEM((8, 2, ROWS, 128), BF16),
            pltpu.VMEM((2, ROWS, 128), BF16),
            pltpu.VMEM((2, ROWS, 128), BF16),
            pltpu.VMEM((4, ROWS, 128), F32),
            pltpu.VMEM((4, ROWS, 128), F32),
            pltpu.VMEM((RATE, 128, ROWS), F32),
            sems((NSEQ,)),
            sems((NSEQ,)),
            sems((NHEAD,)),
            sems((NHEAD,)),
            sems((NHEAD,)),
            sems((NHEAD,)),
            sems((NHEAD,)),
            sems((NHEAD,)),
            sems((NHEAD,)),
            sems((NHEAD,)),
            sems((2,)),
            sems((8,)),
            sems((8,)),
            sems((8,)),
            sems((8,)),
            sems((2,)),
            sems((NSEQ,)),
            sems((NSEQ,)),
            sems((8,)),
            sems((8,)),
            sems((2,)),
        ],
        compiler_params=pltpu.CompilerParams(
            collective_id=0, has_side_effects=True, vmem_limit_bytes=56 * 1024 * 1024
        ),
        cost_estimate=pl.CostEstimate(
            flops=3_000_000_000, bytes_accessed=4_000_000, transcendentals=5_000_000
        ),
    )(
        queries,
        keys,
        values,
        slide_ids.reshape(8, 128),
        head_shift_list,
        out_weight,
        d_y,
    )
    return pl.pallas_call(
        finish,
        out_shape=tuple(jax.ShapeDtypeStruct(r.shape, r.dtype) for r in results),
        in_specs=[vmem] * 5,
        out_specs=(vmem,) * 5,
    )(*results)


def solution(mesh):
    placed = (
        P("seq", "head"),
        P("seq", "head"),
        P("seq", "head"),
        P("seq"),
        P(),
        P("head", None),
        P(("seq", "head"), None),
    )
    return jax.shard_map(
        body,
        mesh=mesh,
        in_specs=placed,
        out_specs=(
            P(("seq", "head"), None),
            P("seq", "head"),
            P("seq", "head"),
            P("seq", "head"),
            P("head", None),
        ),
        check_vma=False,
    )
```

time: 69.2 us -> 62.3 us (0.900)
  local copies, waits for them, and re-layouts: 5.29 us -> 0 us
  Pallas kernels: 63.1 us -> 61.5 us
    unnamed x13 -> x0, local copies, waits for them, and re-layouts: 5.29 us -> none
    pallas_call x1, Pallas kernels: 63.1 us -> 59.3 us  [body(): pl.pallas_call(kernel, out_shape=(jax.ShapeDtypeStruct((128, WIDTH), BF16...]
    pallas_call x0 -> x1, Pallas kernels: none -> 2.2 us  [body(): pl.pallas_call(finish, out_shape=tuple((jax.ShapeDtypeStruct(r.shape, r.d...]
where the time goes in v2:
time: 62.3 us; the launch traced here: 62.1 us
  Pallas kernels  61.5 us (99%)
  between operations  0.64 us (1%)
    pallas_call x1, Pallas kernels, body(): pl.pallas_call(kernel, out_shape=(jax.ShapeDtypeStruct((128, WIDTH), BF16...  59.3 us
    pallas_call x1, Pallas kernels, body(): pl.pallas_call(finish, out_shape=tuple((jax.ShapeDtypeStruct(r.shape, r.d...  2.2 us

profile of v2, /device:TPU:1, one launch (start us, length us, event | category | flops | bytes accessed | tf_op | source)
XLA Modules:
  0.0 62.1 jit_solution(12003863126245188414)
XLA Ops:
  0.6 59.3 %shard_map.110 = (bf16[128,768]{1,0:T(8,128)(2,1)}, bf16[256,384]{1,0:T(8,128)(2,1)}, bf16[256,384]{1,0:T(8,128)(2,1)}, bf16[256,384]{1,0:T(8,128)(2,1)}, bf16[96,768]{1,0:T(8,128)(2,1)}) custom-call(bf16[256,384]{1,0:T(8,128)(2,1)} %q_ref.1, bf16[256,384]{1,0:T(8,128)(2,1)} %k_ref.1, bf16[256,384]{1,0:T(8,128)(2,1)} %v_ref.1, s32[8,128]{1,0:T(8,128)} %bitcast.1, ...), custom_call_target="tpu_custom_call" | custom-call | flops 3000000000 | bytes 4000000 | tf_op jit(solution)/shard_map/pallas_call | solution.py:673
  59.9 2.2 %shard_map.111 = (bf16[128,768]{1,0:T(8,128)(2,1)}, bf16[256,384]{1,0:T(8,128)(2,1)}, bf16[256,384]{1,0:T(8,128)(2,1)}, bf16[256,384]{1,0:T(8,128)(2,1)}, bf16[96,768]{1,0:T(8,128)(2,1)}) custom-call(bf16[128,768]{1,0:T(8,128)(2,1)} %get-tuple-element.10.refs_0_, bf16[256,384]{1,0:T(8,128)(2,1)} %get-tuple-element.11.refs_1_, ...), custom_call_target="tpu_custom_call" | custom-call | tf_op jit(solution)/shard_map/pallas_call | solution.py:759

commit v3 on v2

--- a/solution.py
+++ b/solution.py
@@ -14,6 +14,7 @@
 WIDTH = 768
 NSEQ = 16
 NHEAD = 8
+EARLY = 2
 SAME = 8192.0
 SCALE = 1.0 / math.sqrt(HEAD)
 EXP2 = SCALE * math.log2(math.e)
@@ -57,6 +58,10 @@
     dk_ref,
     dv_ref,
     dw_ref,
+    q_in,
+    k_in,
+    v_in,
+    raw,
     perm,
     near_k,
     near_v,
@@ -89,11 +94,22 @@
     gkv_s,
     gkv_x,
     gkv_r,
-    gkv_p,
-    gkv_y,
+    q_far,
+    q_got,
+    g_far,
+    g_got,
+    o_far,
+    o_got,
+    m_far,
+    m_got,
+    t_far,
+    t_got,
+    dq_far,
+    dq_got,
     acc_k,
     acc_v,
     acc_q,
+    in_sem,
     kv_send,
     kv_recv,
     dy_send,
@@ -114,7 +130,8 @@
     gx_recv,
     g_send,
     g_recv,
-    gy_sem,
+    swap_send,
+    swap_recv,
 ):
     seq = lax.axis_index("seq")
     head = lax.axis_index("head")
@@ -128,6 +145,9 @@
 
     def in_seq(x, dz, c):
         return x * 8 + lax.rem(z + dz, 4) * 2 + c
+
+    def in_z(dz, c):
+        return lax.rem(z + dz, 4) * 2 + c
 
     def in_head(x, dy):
         return x * 4 + lax.rem(y + dy, 4)
@@ -159,6 +179,22 @@
         pl.semaphore_signal(
             barrier, inc=1, device_id={"head": peer_h(i)}, device_id_type=pl.DeviceIdType.MESH
         )
+
+    loads = [
+        pltpu.make_async_copy(source, target, in_sem.at[n])
+        for n, (source, target) in enumerate(
+            (
+                (k_ref, k_in),
+                (v_ref, v_in),
+                (q_ref, q_in),
+                (dy_ref, raw.at[head]),
+                (w_ref.at[0:48], ws.at[head, 0:48]),
+                (w_ref.at[48:96], ws.at[head, 64:112]),
+            )
+        )
+    ]
+    for load in loads:
+        load.start()
 
     slide_col = lax.rem(iota((128, 128), 0), HALF) - HEAD
     below = jnp.zeros((128, 128), F32)
@@ -203,8 +239,20 @@
     for r in range(RATE):
         held = jnp.where(within < HEAD, source + r * HEAD, -1)
         perm[r * 128 : (r + 1) * 128] = jnp.where(given == held, 1.0, 0.0).astype(BF16)
-    k_p = nt(k_ref[...], perm[...])
-    v_p = nt(v_ref[...], perm[...])
+    pl.semaphore_wait(barrier, 15)
+
+    def dy_copy(owner, i, dst, first=False):
+        source = dy_ref if first else raw.at[owner]
+        return remote(source, raw.at[owner], dy_send.at[i], dy_recv.at[owner], "head", dst)
+
+    dy_copy(head, 0, partner_h, True).start()
+    for n, turn in enumerate((2, 1, 3)):
+        dy_copy(head, 1 + n, in_head(x_hi, turn), True).start()
+
+    loads[0].wait()
+    loads[1].wait()
+    k_p = nt(k_in[...], perm[...])
+    v_p = nt(v_in[...], perm[...])
     far_k = jnp.zeros((ROWS, 128), F32)
     far_v = jnp.zeros((ROWS, 128), F32)
     for r in range(RATE):
@@ -216,33 +264,15 @@
         near_v[r] = v_r.astype(BF16)
         far_k = jnp.where(shift_row == r, k_r, far_k)
         far_v = jnp.where(shift_row == r, v_r, far_v)
-    kv[seq, 0] = far_k.astype(BF16)
-    kv[seq, 1] = far_v.astype(BF16)
-
-    rm_row = iota((128, 128), 0)
-    rm_col = iota((128, 128), 1)
-    to_rm = jnp.where(rm_col == lax.rem(rm_row, 32) * RATE + rm_row // 32, 1.0, 0.0).astype(BF16)
-    dy_own = nn(to_rm, dy_ref[...]).astype(BF16)
-    own_rows = pl.ds(pl.multiple_of(head * 32, 32), 32)
-    for r in range(RATE):
-        dys[r, own_rows, :] = dy_own[r * 32 : (r + 1) * 32]
-
-    zeros16 = jnp.zeros((16, WIDTH), BF16)
-    ws[head, 0:48] = w_ref[0:48]
-    ws[head, 64:112] = w_ref[48:96]
-    for h in range(NHEAD):
-        ws[h, 48:64] = zeros16
-        ws[h, 112:128] = zeros16
-
-    pl.semaphore_wait(barrier, 15)
+    own = in_z(0, core)
+    kv[own, 0] = far_k.astype(BF16)
+    kv[own, 1] = far_v.astype(BF16)
 
     def kv_copy(slot, i, dst):
         return remote(kv.at[slot], kv.at[slot], kv_send.at[i], kv_recv.at[slot], "seq", dst)
 
-    def dy_copy(owner, i, dst):
-        rows = pl.ds(pl.multiple_of(owner * 32, 32), 32)
-        part = dys.at[:, rows, :]
-        return remote(part, part, dy_send.at[i], dy_recv.at[owner], "head", dst)
+    def swap(i, source, target):
+        return remote(source, target, swap_send.at[i], swap_recv.at[i], "seq", partner)
 
     def w_copy(owner, i):
         part = ws.at[owner, pl.ds(pl.multiple_of(core * HALF, HALF), HEAD)]
@@ -252,16 +282,12 @@
         part = ws.at[owner, pl.ds(pl.multiple_of(half * HALF, HALF), HEAD)]
         return remote(part, part, ws_send.at[owner], ws_recv.at[owner], "seq", sibling)
 
-    kv_copy(seq, 0, partner).start()
-    for j, turn in enumerate(turns):
-        kv_copy(seq, 1 + j, in_seq(x_lo, turn, core)).start()
-    kv_copy(seq, 4, sibling).start()
-    dy_copy(head, 0, partner_h).start()
     for n, turn in enumerate(turns):
-        dy_copy(head, 1 + n, in_head(x_hi, turn)).start()
-
-    q_p = nt(q_ref[...], perm[...])
-    q_pt = nt(perm[...], q_ref[...])
+        kv_copy(own, n, in_seq(x_lo, turn, core)).start()
+    kv_copy(own, 3, sibling).start()
+    loads[2].wait()
+    q_p = nt(q_in[...], perm[...])
+    q_pt = nt(perm[...], q_in[...])
     q_rows = []
     q_cols = []
     for r in range(RATE):
@@ -269,11 +295,16 @@
         hot = jnp.where(hot_col & (at >= first_col) & (at < last_col), SAME, 0.0)
         q_rows.append(q_p[:, r * 128 : (r + 1) * 128])
         q_cols.append(q_pt[r * 128 : (r + 1) * 128, :] + hot)
-    for j in range(RATE):
+    for j in reversed(range(RATE)):
         q_j = to_slot(q_rows, shift_row, j)
         q_jt = to_slot(q_cols, shift_col, j)
         q_n[0, j] = jnp.where(lane_row < HALF, q_j, 0.0).astype(BF16)
         q_n[1, j] = jnp.where(lane_row < HALF, 0.0, q_j).astype(BF16)
+        if j == 3:
+            at = (iota((ROWS, 128), 0) * RATE + shift_row).astype(F32)
+            hot = jnp.where(hot_row & (at >= first_row) & (at < last_row), SAME, 0.0)
+            q_far[...] = (q_j + hot).astype(BF16)
+            swap(0, q_far, q_got).start()
         q_t[0, j] = jnp.where(lane_col < HALF, q_jt, 0.0).astype(BF16)
         q_t[1, j] = jnp.where(lane_col < HALF, 0.0, q_jt).astype(BF16)
 
@@ -311,111 +342,158 @@
 
         @pl.when(j == 0)
         def _():
-            kv_copy(partner, 0, partner).wait_recv()
-            for n, turn in enumerate(turns):
-                kv_copy(partner, 5 + n, in_seq(x_lo, turn, core)).start()
-            kv_copy(partner, 8, sibling).start()
-
-        @pl.when(j == 1)
+            dy_copy(partner_h, 0, partner_h).wait_recv()
+            for n, turn in enumerate((1, 3)):
+                dy_copy(partner_h, 4 + n, in_head(x_hi, turn)).start()
+
+    def share(i):
+        slot = in_z(i + i // 2 - 2 * (i // 3), core)
+        kv_copy(slot, 0, partner).wait_recv()
+        kv_copy(slot, 3 + i, sibling).start()
+
+    share(1)
+    swap(0, q_far, q_got).wait_recv()
+    q_j = q_got[...].astype(F32)
+    q_jt = q_j.T
+    q_n[0, 4] = jnp.where(lane_row < HALF, q_j, 0.0).astype(BF16)
+    q_n[1, 4] = jnp.where(lane_row < HALF, 0.0, q_j).astype(BF16)
+    q_t[0, 4] = jnp.where(lane_col < HALF, q_jt, 0.0).astype(BF16)
+    q_t[1, 4] = jnp.where(lane_col < HALF, 0.0, q_jt).astype(BF16)
+
+    def far_block(n):
+        i = n // 2
+        return in_z(i + i // 2 - 2 * (i // 3), lax.rem(n, 2))
+
+    kv_copy(in_z(0, 1 - core), 0, partner).wait_recv()
+    kv_copy(in_z(1, 1 - core), 0, partner).wait_recv()
+
+    @pl.loop(0, 4)
+    def _(step):
+        g = lax.rem(step, 2)
+        own_q = step // 2
+
+        @pl.when(step == 1)
         def _():
-            dy_copy(partner_h, 0, partner_h).wait_recv()
-            for n, turn in enumerate(turns):
-                dy_copy(partner_h, 4 + n, in_head(x_hi, turn)).start()
-
-    def share(i):
-        dz = i + i // 2 - 2 * (i // 3)
-        for x in range(2):
-            slot = in_seq(x, dz, core)
-            kv_copy(slot, 0, partner).wait_recv()
-            kv_copy(slot, 9 + 2 * (i - 1) + x, sibling).start()
-
-    def far_forward(i):
-        dz = i + i // 2 - 2 * (i // 3)
-        for x in range(2):
-            kv_copy(in_seq(x, dz, 1 - core), 0, partner).wait_recv()
+            dy_copy(in_head(x_hi, 2), 0, partner_h).wait_recv()
+            dy_copy(in_head(x_hi, 2), 6, partner_h).start()
+            for i in (2, 3):
+                share(i)
+            for dz in (3, 2):
+                kv_copy(in_z(dz, 1 - core), 0, partner).wait_recv()
+
+        @pl.when(step == 2)
+        def _():
+            for h in range(2):
+                top = jnp.maximum(top_f[0, h, 0], top_f[0, h, 1])
+                w0 = jnp.exp2((top_f[0, h, 0] - top) * EXP2)
+                w1 = jnp.exp2((top_f[0, h, 1] - top) * EXP2)
+                m_far[h : h + 1] = top
+                m_far[2 + h : 3 + h] = w0 * sum_f[0, h, 0] + w1 * sum_f[0, h, 1]
+                o_far[halves[h]] = (w0 * out_f[0, h, 0] + w1 * out_f[0, h, 1]).astype(BF16)
+            m_far[4:8] = jnp.zeros((4, ROWS), F32)
+            swap(1, m_far, m_got).start()
+            swap(2, o_far, o_got).start()
+
         for h in range(2):
             top, total, out = forward(
-                lambda b: kv[in_seq(b // 2, dz, b % 2), 0],
-                lambda b: kv[in_seq(b // 2, dz, b % 2), 1],
-                q_t[h, 3],
-                e_far.at[h, i],
+                lambda b: kv[far_block(4 * g + b), 0],
+                lambda b: kv[far_block(4 * g + b), 1],
+                q_t[h, 4 - own_q],
+                e_far.at[own_q, h, pl.ds(4 * g, 4)],
                 h,
             )
-            top_f[h, i] = top
-            sum_f[h, i] = total
-            out_f[h, i] = out
-
-    @pl.loop(0, 4)
-    def _(i):
-        @pl.when(i == 1)
-        def _():
-            share(1)
-
-        @pl.when((i == 1) | (i == 2))
-        def _():
-            share(i + 1)
-
-        far_forward(i)
-
-    for h in range(2):
-        top = top_n[h]
-        for i in range(4):
-            top = jnp.maximum(top, top_f[h, i])
-        weight = jnp.exp2((top_n[h] - top) * EXP2)
-        total = weight * sum_n[h]
-        out = weight * out_n[h]
-        weights = []
-        for i in range(4):
-            w_i = jnp.exp2((top_f[h, i] - top) * EXP2)
-            weights.append(w_i)
-            total = total + w_i * sum_f[h, i]
-            out = out + w_i * out_f[h, i]
-        inverse = 1.0 / total
-        fac_n[h, 3] = weight * inverse
-        for i in range(4):
-            fac_f[h, i] = weights[i] * inverse
-        attn_t[3, halves[h]] = (out * inverse).astype(BF16)
-
-    attn_slots = [attn_t[j].astype(F32) for j in range(RATE)]
-    attn_rt = [from_slot(attn_slots, shift_col, r) for r in range(RATE)]
-    for r in range(RATE):
-        attn_n[r] = attn_rt[r].T.astype(BF16)
-
-    def at_copy(slot, i):
-        rows = pl.ds(pl.multiple_of(peer_h(i) * 32, 32), 32)
-        return remote(
-            attn_n.at[:, rows, :], attn_r.at[slot], at_send.at[i], at_recv.at[slot], "head", peer_h(i)
-        )
-
-    for n in range(1, NHEAD):
-        at_copy(head, n).start()
-    for r in range(RATE):
-        attn_r[head, r] = attn_n[r, own_rows, :]
-
-    for turn in turns:
+            top_f[own_q, h, g] = top
+            sum_f[own_q, h, g] = total
+            out_f[own_q, h, g] = out
+
+    for turn in (1, 3):
         for x in range(2):
             dy_copy(in_head(x, turn), 0, partner_h).wait_recv()
-    for n in range(1, NHEAD):
-        w_copy(head, n).start()
-
+    dy_copy(in_head(1 - x_hi, 2), 0, partner_h).wait_recv()
+    loads[3].wait()
+    loads[4].wait()
+    loads[5].wait()
+    zeros16 = jnp.zeros((16, WIDTH), BF16)
+    for h in range(NHEAD):
+        ws[h, 48:64] = zeros16
+        ws[h, 112:128] = zeros16
+    rm_row = iota((128, 128), 0)
+    rm_col = iota((128, 128), 1)
+    to_rm = jnp.where(rm_col == lax.rem(rm_row, 32) * RATE + rm_row // 32, 1.0, 0.0).astype(BF16)
+
+    for h in range(NHEAD):
+        rows = nn(to_rm, raw[h]).astype(BF16)
+        for r in range(RATE):
+            dys[r, h * 32 : (h + 1) * 32] = rows[r * 32 : (r + 1) * 32]
     w_own = ws[head]
     g_rows = []
     g_cols = []
-    weight_grad = jnp.zeros((128, WIDTH), F32)
     for r in range(RATE):
         g_rows.append(nt(dys[r], w_own))
         g_cols.append(nt(w_own, dys[r]))
-        weight_grad = weight_grad + nn(attn_rt[r].astype(BF16), dys[r])
-    for j in range(RATE):
+    for j in reversed(range(RATE)):
         g_j = to_slot(g_rows, shift_row, j)
         g_jt = to_slot(g_cols, shift_col, j)
         g_n[0, j] = jnp.where(lane_row < HALF, g_j, 0.0).astype(BF16)
         g_n[1, j] = jnp.where(lane_row < HALF, 0.0, g_j).astype(BF16)
         g_t[0, j] = jnp.where(lane_col < HALF, g_jt, 0.0).astype(BF16)
         g_t[1, j] = jnp.where(lane_col < HALF, 0.0, g_jt).astype(BF16)
+        if j == 3:
+            g_far[...] = g_j.astype(BF16)
+            swap(3, g_far, g_got).start()
+    swap(1, m_far, m_got).wait_recv()
+    swap(2, o_far, o_got).wait_recv()
+    for h in range(2):
+        tops = [top_n[h], top_f[1, h, 0], top_f[1, h, 1], m_got[h : h + 1]]
+        sums = [sum_n[h], sum_f[1, h, 0], sum_f[1, h, 1], m_got[2 + h : 3 + h]]
+        outs = [out_n[h], out_f[1, h, 0], out_f[1, h, 1], o_got[halves[h]].astype(F32)]
+        top = tops[0]
+        for other in tops[1:]:
+            top = jnp.maximum(top, other)
+        weights = [jnp.exp2((other - top) * EXP2) for other in tops]
+        total = weights[0] * sums[0]
+        out = weights[0] * outs[0]
+        for n in range(1, 4):
+            total = total + weights[n] * sums[n]
+            out = out + weights[n] * outs[n]
+        inverse = 1.0 / total
+        fac_n[h, 3] = weights[0] * inverse
+        for g in range(2):
+            fac_f[1, h, g] = weights[1 + g] * inverse
+        t_far[h : h + 1] = top
+        t_far[2 + h : 3 + h] = inverse
+        attn_t[3, halves[h]] = (out * inverse).astype(BF16)
+
+    for j in range(RATE):
         for h in range(2):
             product = g_t[h, j, halves[h], :].astype(F32) * attn_t[j, halves[h]].astype(F32)
             delta[h, j] = jnp.sum(product, axis=0, keepdims=True)
+    t_far[4:5] = delta[0, 3]
+    t_far[5:6] = delta[1, 3]
+    t_far[6:8] = jnp.zeros((2, ROWS), F32)
+    swap(4, t_far, t_got).start()
+
+    attn_slots = [attn_t[j].astype(F32) for j in range(RATE)]
+    attn_rt = [from_slot(attn_slots, shift_col, r) for r in range(RATE)]
+    for r in range(RATE):
+        attn_n[r] = attn_rt[r].T.astype(BF16)
+
+    own_rows = pl.ds(pl.multiple_of(head * 32, 32), 32)
+
+    def at_copy(slot, i):
+        rows = pl.ds(pl.multiple_of(peer_h(i) * 32, 32), 32)
+        return remote(
+            attn_n.at[:, rows, :], attn_r.at[slot], at_send.at[i], at_recv.at[slot], "head", peer_h(i)
+        )
+
+    for n in range(1, NHEAD):
+        at_copy(head, n).start()
+    for r in range(RATE):
+        attn_r[head, r] = attn_n[r, own_rows, :]
+
+    weight_grad = jnp.zeros((128, WIDTH), F32)
+    for r in range(RATE):
+        weight_grad = weight_grad + nn(attn_rt[r].astype(BF16), dys[r])
 
     for half in range(2):
         for n in range(8):
@@ -459,19 +537,20 @@
             df_copy(peer_c(n), n).wait_recv()
         dc_copy(core).start()
 
-    def backward(keys, vals, j, e_of, factor, put):
-        dq = [jnp.zeros((HALF, ROWS), F32), jnp.zeros((HALF, ROWS), F32)]
-        for b in range(4):
+    def backward(count, keys, vals, queries, e_of, factor, put):
+        dq = [[jnp.zeros((HALF, ROWS), F32) for h in range(2)] for _ in queries]
+        for b in range(count):
             k_t = keys(b).T
             val = vals(b)
             dk = jnp.zeros((ROWS, 128), F32)
             dv = jnp.zeros((ROWS, 128), F32)
-            for h in range(2):
-                p = e_of(h)[b] * factor(h)
-                ds = (p * (nn(val, g_t[h, j]) - delta[h, j])).astype(BF16)
-                dv = dv + nn(p.astype(BF16), g_n[h, j])
-                dk = dk + nn(ds, q_n[h, j])
-                dq[h] = dq[h] + nn(k_t[halves[h]], ds)
+            for n, j in enumerate(queries):
+                for h in range(2):
+                    p = e_of(n, h, b) * factor(n, h)
+                    ds = (p * (nn(val, g_t[h, j]) - delta[h, j])).astype(BF16)
+                    dv = dv + nn(p.astype(BF16), g_n[h, j])
+                    dk = dk + nn(ds, q_n[h, j])
+                    dq[n][h] = dq[n][h] + nn(k_t[halves[h]], ds)
             put(b, dk, dv)
         return dq
 
@@ -484,61 +563,67 @@
             acc_v[b] = acc_v[b] + dv
 
         dq = backward(
+            4,
             lambda b: near_k[b],
             lambda b: near_v[b],
-            j,
-            lambda h: e_near.at[h, j],
-            lambda h: fac_n[h, j],
+            [j],
+            lambda n, h, b: e_near[h, j, b],
+            lambda n, h: fac_n[h, j],
             put,
         )
         for h in range(2):
-            acc_q[j, halves[h]] = dq[h]
+            acc_q[j, halves[h]] = dq[0][h]
+
+    @pl.loop(0, EARLY)
+    def _(j):
+        near_backward(j)
+
+        @pl.when(j == 0)
+        def _():
+            weight_over_cores()
+
+    swap(3, g_far, g_got).wait_recv()
+    swap(4, t_far, t_got).wait_recv()
+    g_j = g_got[...].astype(F32)
+    g_jt = g_j.T
+    g_n[0, 4] = jnp.where(lane_row < HALF, g_j, 0.0).astype(BF16)
+    g_n[1, 4] = jnp.where(lane_row < HALF, 0.0, g_j).astype(BF16)
+    g_t[0, 4] = jnp.where(lane_col < HALF, g_jt, 0.0).astype(BF16)
+    g_t[1, 4] = jnp.where(lane_col < HALF, 0.0, g_jt).astype(BF16)
+    for h in range(2):
+        delta[h, 4] = t_got[4 + h : 5 + h]
+        for g in range(2):
+            weight = jnp.exp2((top_f[0, h, g] - t_got[h : h + 1]) * EXP2)
+            fac_f[0, h, g] = weight * t_got[2 + h : 3 + h]
 
     def gx_copy(slot):
         return remote(
             gkv_s.at[slot], gkv_x.at[slot], gx_send.at[slot], gx_recv.at[slot], "seq", sibling
         )
 
-    def grad_copy(x, dz):
-        slot = in_seq(x, dz, core)
-        index = dz + 4 * (x != x_lo)
+    def grad_copy(dz):
         return remote(
-            gkv_s.at[slot],
-            gkv_r.at[index],
-            g_send.at[index],
-            g_recv.at[index],
+            gkv_s.at[in_z(dz, core)],
+            gkv_r.at[dz],
+            g_send.at[dz],
+            g_recv.at[dz],
             "seq",
             in_seq(x_lo, dz, core),
         )
 
-    def gy_copy():
-        return remote(gkv_p, gkv_y, gy_sem.at[0], gy_sem.at[1], "seq", partner)
-
     def merge(i):
         dz = i + i // 2 - 2 * (i // 3)
-        for x in range(2):
-            slot = in_seq(x, dz, core)
-            gx_copy(slot).wait_recv()
-            for n in range(2):
-                gkv_s[slot, n] = (
-                    gkv_s[slot, n].astype(F32) + gkv_x[slot, n].astype(F32)
-                ).astype(BF16)
-
-            @pl.when(dz != 0)
-            def _():
-                grad_copy(x, dz).start()
-
-    def sum_partner():
-        for turn in turns:
-            grad_copy(1 - x_lo, turn).wait_recv()
+        slot = in_z(dz, core)
+        gx_copy(slot).wait_recv()
         for n in range(2):
-            total = gkv_s[partner, n].astype(F32)
-            for turn in turns:
-                total = total + gkv_r[4 + turn, n].astype(F32)
-            gkv_p[n] = total.astype(BF16)
-        gy_copy().start()
-
-    acc_q[3] = jnp.zeros((128, ROWS), F32)
+            gkv_s[slot, n] = (gkv_s[slot, n].astype(F32) + gkv_x[slot, n].astype(F32)).astype(BF16)
+
+        @pl.when(dz != 0)
+        def _():
+            grad_copy(dz).start()
+
+    for j in (3, 4):
+        acc_q[j] = jnp.zeros((128, ROWS), F32)
 
     @pl.loop(0, 4)
     def _(back):
@@ -546,24 +631,26 @@
         dz = i + i // 2 - 2 * (i // 3)
 
         def put(b, dk, dv):
-            slot = in_seq(b // 2, dz, b % 2)
+            slot = in_z(dz, b)
             gkv_s[slot, 0] = dk.astype(BF16)
             gkv_s[slot, 1] = dv.astype(BF16)
 
-            @pl.when(core != b % 2)
+            @pl.when(core != b)
             def _():
                 gx_copy(slot).start()
 
         dq = backward(
-            lambda b: kv[in_seq(b // 2, dz, b % 2), 0],
-            lambda b: kv[in_seq(b // 2, dz, b % 2), 1],
-            3,
-            lambda h: e_far.at[h, i],
-            lambda h: fac_f[h, i],
+            2,
+            lambda b: kv[in_z(dz, b), 0],
+            lambda b: kv[in_z(dz, b), 1],
+            [4, 3],
+            lambda n, h, b: e_far[n, h, 2 * i + b],
+            lambda n, h: fac_f[n, h, i // 2],
             put,
         )
-        for h in range(2):
-            acc_q[3, halves[h]] = acc_q[3, halves[h]] + dq[h]
+        for n, j in enumerate((4, 3)):
+            for h in range(2):
+                acc_q[j, halves[h]] = acc_q[j, halves[h]] + dq[n][h]
 
         @pl.when(back > 0)
         def _():
@@ -571,35 +658,32 @@
 
         @pl.when(back == 0)
         def _():
-            weight_over_cores()
-
-        @pl.when(back == 3)
+            for n in range(1, NHEAD):
+                w_copy(head, n).start()
+
+        @pl.when(back == 2)
         def _():
             weight_over_chips()
 
-    acc_far = acc_q[3]
+    dq_far[...] = acc_q[4].astype(BF16)
+    swap(5, dq_far, dq_got).start()
+    acc_q[4] = acc_q[3]
     merge(0)
 
-    @pl.loop(0, RATE)
+    @pl.loop(EARLY, RATE)
     def _(j):
         near_backward(j)
 
-        @pl.when(j == 1)
-        def _():
-            weight_to_sibling()
-            for n in range(1, NHEAD):
-                w_copy(peer_h(n), n).wait_recv()
-                w_share(peer_h(n), core).start()
-
-        @pl.when(j == 2)
-        def _():
-            sum_partner()
-
-    acc_q[3] = acc_q[3] + acc_far
+    for n in range(1, NHEAD):
+        w_copy(peer_h(n), n).wait_recv()
+        w_share(peer_h(n), core).start()
+    swap(5, dq_far, dq_got).wait_recv()
+    acc_q[3] = acc_q[3] + acc_q[4] + dq_got[...].astype(F32)
     dq_slots = [(acc_q[j] * SCALE).T for j in range(RATE)]
     dq_parts = [from_slot(dq_slots, shift_row, r).astype(BF16) for r in range(RATE)]
     dq_ref[...] = nn(jnp.concatenate(dq_parts, axis=1), perm[...]).astype(BF16)
 
+    weight_to_sibling()
     for n in range(1, NHEAD):
         w_share(peer_h(n), 1 - core).wait_recv()
         at_copy(peer_h(n), n).wait_recv()
@@ -611,11 +695,10 @@
     lo_ref[...] = result.astype(BF16)
 
     for turn in turns:
-        grad_copy(x_lo, turn).wait_recv()
-    gy_copy().wait_recv()
+        grad_copy(turn).wait_recv()
     far = []
     for n in range(2):
-        total = gkv_s[seq, n].astype(F32) + gkv_y[n].astype(F32)
+        total = gkv_s[own, n].astype(F32)
         for turn in turns:
             total = total + gkv_r[turn, n].astype(F32)
         far.append(total)
@@ -638,9 +721,9 @@
     dx_copy(1 - core).wait_send()
     dc_copy(core).wait_send()
 
-    @pl.loop(0, 15)
+    @pl.loop(0, 7)
     def _(i):
-        kv_copy(seq, i, partner).wait_send()
+        kv_copy(own, i, partner).wait_send()
 
     @pl.loop(1, 8)
     def _(i):
@@ -651,14 +734,15 @@
         dw_copy(chip, i).wait_send()
         df_copy(chip, i).wait_send()
 
-    @pl.loop(0, 8)
+    @pl.loop(0, 4)
     def _(i):
         gx_copy(i * 2 + 1 - core).wait_send()
 
-    gy_copy().wait_send()
     for turn in turns:
-        for x in range(2):
-            grad_copy(x, turn).wait_send()
+        grad_copy(turn).wait_send()
+    swaps = ((q_far, q_got), (m_far, m_got), (o_far, o_got), (g_far, g_got), (t_far, t_got), (dq_far, dq_got))
+    for i, (source, target) in enumerate(swaps):
+        swap(i, source, target).wait_send()
 
 
 def finish(*refs):
@@ -668,6 +752,7 @@
 
 def body(queries, keys, values, slide_ids, head_shift_list, out_weight, d_y):
     vmem = pl.BlockSpec(memory_space=pltpu.VMEM)
+    hbm = pl.BlockSpec(memory_space=pltpu.HBM)
     smem = pl.BlockSpec(memory_space=pltpu.SMEM)
     sems = pltpu.SemaphoreType.DMA
     results = pl.pallas_call(
@@ -679,28 +764,32 @@
             jax.ShapeDtypeStruct((ROWS, 384), BF16),
             jax.ShapeDtypeStruct((96, WIDTH), BF16),
         ),
-        in_specs=[vmem, vmem, vmem, vmem, smem, vmem, vmem],
+        in_specs=[hbm, hbm, hbm, vmem, smem, hbm, hbm],
         out_specs=(vmem,) * 5,
         scratch_shapes=[
+            pltpu.VMEM((ROWS, 384), BF16),
+            pltpu.VMEM((ROWS, 384), BF16),
+            pltpu.VMEM((ROWS, 384), BF16),
+            pltpu.VMEM((NHEAD, 128, WIDTH), BF16),
             pltpu.VMEM((4 * 128, 384), BF16),
             pltpu.VMEM((4, ROWS, 128), BF16),
             pltpu.VMEM((4, ROWS, 128), BF16),
-            pltpu.VMEM((NSEQ, 2, ROWS, 128), BF16),
-            pltpu.VMEM((2, RATE, 128, ROWS), BF16),
-            pltpu.VMEM((2, RATE, ROWS, 128), BF16),
-            pltpu.VMEM((2, RATE, 128, ROWS), BF16),
-            pltpu.VMEM((2, RATE, ROWS, 128), BF16),
+            pltpu.VMEM((8, 2, ROWS, 128), BF16),
+            pltpu.VMEM((2, 5, 128, ROWS), BF16),
+            pltpu.VMEM((2, 5, ROWS, 128), BF16),
+            pltpu.VMEM((2, 5, 128, ROWS), BF16),
+            pltpu.VMEM((2, 5, ROWS, 128), BF16),
             pltpu.VMEM((2, RATE, 4, ROWS, ROWS), F32),
-            pltpu.VMEM((2, 4, 4, ROWS, ROWS), F32),
+            pltpu.VMEM((2, 2, 8, ROWS, ROWS), F32),
             pltpu.VMEM((2, 1, ROWS), F32),
             pltpu.VMEM((2, 1, ROWS), F32),
             pltpu.VMEM((2, HALF, ROWS), F32),
-            pltpu.VMEM((2, 4, 1, ROWS), F32),
-            pltpu.VMEM((2, 4, 1, ROWS), F32),
-            pltpu.VMEM((2, 4, HALF, ROWS), F32),
+            pltpu.VMEM((2, 2, 2, 1, ROWS), F32),
+            pltpu.VMEM((2, 2, 2, 1, ROWS), F32),
+            pltpu.VMEM((2, 2, 2, HALF, ROWS), F32),
             pltpu.VMEM((2, RATE, 1, ROWS), F32),
-            pltpu.VMEM((2, 4, 1, ROWS), F32),
-            pltpu.VMEM((2, RATE, 1, ROWS), F32),
+            pltpu.VMEM((2, 2, 2, 1, ROWS), F32),
+            pltpu.VMEM((2, 5, 1, ROWS), F32),
             pltpu.VMEM((RATE, 128, ROWS), BF16),
             pltpu.VMEM((RATE, ROWS, 128), BF16),
             pltpu.VMEM((NHEAD, RATE, 32, 128), BF16),
@@ -711,16 +800,27 @@
             pltpu.VMEM((8, 16, 384), F32),
             pltpu.VMEM((8, 16, 384), F32),
             pltpu.VMEM((2, 8, 16, 384), BF16),
-            pltpu.VMEM((NSEQ, 2, ROWS, 128), BF16),
-            pltpu.VMEM((NSEQ, 2, ROWS, 128), BF16),
             pltpu.VMEM((8, 2, ROWS, 128), BF16),
-            pltpu.VMEM((2, ROWS, 128), BF16),
-            pltpu.VMEM((2, ROWS, 128), BF16),
+            pltpu.VMEM((8, 2, ROWS, 128), BF16),
+            pltpu.VMEM((4, 2, ROWS, 128), BF16),
+            pltpu.VMEM((ROWS, 128), BF16),
+            pltpu.VMEM((ROWS, 128), BF16),
+            pltpu.VMEM((ROWS, 128), BF16),
+            pltpu.VMEM((ROWS, 128), BF16),
+            pltpu.VMEM((128, ROWS), BF16),
+            pltpu.VMEM((128, ROWS), BF16),
+            pltpu.VMEM((8, ROWS), F32),
+            pltpu.VMEM((8, ROWS), F32),
+            pltpu.VMEM((8, ROWS), F32),
+            pltpu.VMEM((8, ROWS), F32),
+            pltpu.VMEM((128, ROWS), BF16),
+            pltpu.VMEM((128, ROWS), BF16),
             pltpu.VMEM((4, ROWS, 128), F32),
             pltpu.VMEM((4, ROWS, 128), F32),
-            pltpu.VMEM((RATE, 128, ROWS), F32),
-            sems((NSEQ,)),
-            sems((NSEQ,)),
+            pltpu.VMEM((5, 128, ROWS), F32),
+            sems((6,)),
+            sems((8,)),
+            sems((8,)),
             sems((NHEAD,)),
             sems((NHEAD,)),
             sems((NHEAD,)),
@@ -735,11 +835,12 @@
             sems((8,)),
             sems((8,)),
             sems((2,)),
-            sems((NSEQ,)),
-            sems((NSEQ,)),
             sems((8,)),
             sems((8,)),
-            sems((2,)),
+            sems((4,)),
+            sems((4,)),
+            sems((6,)),
+            sems((6,)),
         ],
         compiler_params=pltpu.CompilerParams(
             collective_id=0, has_side_effects=True, vmem_limit_bytes=56 * 1024 * 1024

time: 62.3 us -> 55.7 us (0.89)
  Pallas kernels: 61.5 us -> 54.9 us
    pallas_call x1, Pallas kernels: 59.3 us -> 52.7 us  [body(): pl.pallas_call(kernel, out_shape=(jax.ShapeDtypeStruct((128, WIDTH), BF16...]
where the time goes in v3:
time: 55.7 us; the launch traced here: 55.5 us
  Pallas kernels  54.9 us (99%)
  between operations  0.64 us (1%)
    pallas_call x1, Pallas kernels, body(): pl.pallas_call(kernel, out_shape=(jax.ShapeDtypeStruct((128, WIDTH), BF16...  52.7 us
    pallas_call x1, Pallas kernels, body(): pl.pallas_call(finish, out_shape=tuple((jax.ShapeDtypeStruct(r.shape, r.d...  2.2 us

profile of v3, /device:TPU:1, one launch (start us, length us, event | category | flops | bytes accessed | tf_op | source)
XLA Modules:
  0.0 55.5 jit_solution(8222673360587844554)
XLA Ops:
  0.6 52.7 %shard_map.110 = (bf16[128,768]{1,0:T(8,128)(2,1)}, bf16[256,384]{1,0:T(8,128)(2,1)}, bf16[256,384]{1,0:T(8,128)(2,1)}, bf16[256,384]{1,0:T(8,128)(2,1)}, bf16[96,768]{1,0:T(8,128)(2,1)}) custom-call(bf16[256,384]{1,0:T(8,128)(2,1)} %q_ref.1, bf16[256,384]{1,0:T(8,128)(2,1)} %k_ref.1, bf16[256,384]{1,0:T(8,128)(2,1)} %v_ref.1, s32[8,128]{1,0:T(8,128)} %bitcast.1, ...), custom_call_target="tpu_custom_call" | custom-call | flops 3000000000 | bytes 4000000 | tf_op jit(solution)/shard_map/pallas_call | solution.py:758
  53.3 2.2 %shard_map.111 = (bf16[128,768]{1,0:T(8,128)(2,1)}, bf16[256,384]{1,0:T(8,128)(2,1)}, bf16[256,384]{1,0:T(8,128)(2,1)}, bf16[256,384]{1,0:T(8,128)(2,1)}, bf16[96,768]{1,0:T(8,128)(2,1)}) custom-call(bf16[128,768]{1,0:T(8,128)(2,1)} %get-tuple-element.10.refs_0_, bf16[256,384]{1,0:T(8,128)(2,1)} %get-tuple-element.11.refs_1_, ...), custom_call_target="tpu_custom_call" | custom-call | tf_op jit(solution)/shard_map/pallas_call | solution.py:860

commit v4 on v3

--- a/solution.py
+++ b/solution.py
@@ -65,7 +65,11 @@
     perm,
     near_k,
     near_v,
+    near_kt,
+    near_vt,
     kv,
+    far_vt,
+    g_raw,
     q_t,
     q_n,
     g_t,
@@ -246,20 +250,21 @@
         return remote(source, raw.at[owner], dy_send.at[i], dy_recv.at[owner], "head", dst)
 
     dy_copy(head, 0, partner_h, True).start()
-    for n, turn in enumerate((2, 1, 3)):
-        dy_copy(head, 1 + n, in_head(x_hi, turn), True).start()
+    dy_copy(head, 1, in_head(x_hi, 2), True).start()
 
     loads[0].wait()
     loads[1].wait()
     k_p = nt(k_in[...], perm[...])
     v_p = nt(v_in[...], perm[...])
+    one_row = jnp.where(lax.rem(lane_row, HALF) == HEAD, 1.0, 0.0)
+    one_col = jnp.where(lax.rem(lane_col, HALF) == HEAD, 1.0, 0.0)
     far_k = jnp.zeros((ROWS, 128), F32)
     far_v = jnp.zeros((ROWS, 128), F32)
     for r in range(RATE):
         at = (iota((ROWS, 128), 0) * RATE + r).astype(F32)
         hot = jnp.where(hot_row & (at >= first_row) & (at < last_row), 1.0, 0.0)
         k_r = k_p[:, r * 128 : (r + 1) * 128] + hot
-        v_r = v_p[:, r * 128 : (r + 1) * 128]
+        v_r = v_p[:, r * 128 : (r + 1) * 128] + one_row
         near_k[r] = k_r.astype(BF16)
         near_v[r] = v_r.astype(BF16)
         far_k = jnp.where(shift_row == r, k_r, far_k)
@@ -285,9 +290,16 @@
     for n, turn in enumerate(turns):
         kv_copy(own, n, in_seq(x_lo, turn, core)).start()
     kv_copy(own, 3, sibling).start()
+    for n, turn in enumerate((1, 3)):
+        dy_copy(head, 2 + n, in_head(x_hi, turn), True).start()
     loads[2].wait()
     q_p = nt(q_in[...], perm[...])
     q_pt = nt(perm[...], q_in[...])
+    k_pt = nt(perm[...], k_in[...])
+    v_pt = nt(perm[...], v_in[...])
+    for r in range(RATE):
+        near_kt[r] = k_pt[r * 128 : (r + 1) * 128].astype(BF16)
+        near_vt[r] = (v_pt[r * 128 : (r + 1) * 128] + one_col).astype(BF16)
     q_rows = []
     q_cols = []
     for r in range(RATE):
@@ -308,22 +320,19 @@
         q_t[0, j] = jnp.where(lane_col < HALF, q_jt, 0.0).astype(BF16)
         q_t[1, j] = jnp.where(lane_col < HALF, 0.0, q_jt).astype(BF16)
 
-    def forward(keys, vals, q_of, e_of, h):
+    def forward(keys, vals_t, q_of, e_of, h):
         top = None
         for b in range(4):
             s = nn(keys(b), q_of)
             e_of[b] = s
             m = jnp.max(s, axis=0, keepdims=True)
             top = m if top is None else jnp.maximum(top, m)
-        total = jnp.zeros((1, ROWS), F32)
         out = jnp.zeros((HALF, ROWS), F32)
         for b in range(4):
             e = jnp.exp2((e_of[b] - top) * EXP2)
             e_of[b] = e
-            total = total + jnp.sum(e, axis=0, keepdims=True)
-            v_t = vals(b).T[h * HALF : (h + 1) * HALF]
-            out = out + nn(v_t, e.astype(BF16))
-        return top, total, out
+            out = out + nn(vals_t(b)[h * HALF : (h + 1) * HALF], e.astype(BF16))
+        return top, out[HEAD : HEAD + 1], out
 
     halves = (slice(0, HALF), slice(HALF, 2 * HALF))
 
@@ -331,7 +340,7 @@
     def _(j):
         for h in range(2):
             top, total, out = forward(
-                lambda b: near_k[b], lambda b: near_v[b], q_t[h, j], e_near.at[h, j], h
+                lambda b: near_k[b], lambda b: near_vt[b], q_t[h, j], e_near.at[h, j], h
             )
             top_n[h] = top
             sum_n[h] = total
@@ -345,6 +354,8 @@
             dy_copy(partner_h, 0, partner_h).wait_recv()
             for n, turn in enumerate((1, 3)):
                 dy_copy(partner_h, 4 + n, in_head(x_hi, turn)).start()
+            dy_copy(in_head(x_hi, 2), 0, partner_h).wait_recv()
+            dy_copy(in_head(x_hi, 2), 6, partner_h).start()
 
     def share(i):
         slot = in_z(i + i // 2 - 2 * (i // 3), core)
@@ -367,6 +378,12 @@
     kv_copy(in_z(0, 1 - core), 0, partner).wait_recv()
     kv_copy(in_z(1, 1 - core), 0, partner).wait_recv()
 
+    def turn_values(g):
+        for b in range(4):
+            far_vt[4 * g + b] = kv[far_block(4 * g + b), 1].T
+
+    turn_values(0)
+
     @pl.loop(0, 4)
     def _(step):
         g = lax.rem(step, 2)
@@ -374,12 +391,11 @@
 
         @pl.when(step == 1)
         def _():
-            dy_copy(in_head(x_hi, 2), 0, partner_h).wait_recv()
-            dy_copy(in_head(x_hi, 2), 6, partner_h).start()
             for i in (2, 3):
                 share(i)
             for dz in (3, 2):
                 kv_copy(in_z(dz, 1 - core), 0, partner).wait_recv()
+            turn_values(1)
 
         @pl.when(step == 2)
         def _():
@@ -397,7 +413,7 @@
         for h in range(2):
             top, total, out = forward(
                 lambda b: kv[far_block(4 * g + b), 0],
-                lambda b: kv[far_block(4 * g + b), 1],
+                lambda b: far_vt[4 * g + b],
                 q_t[h, 4 - own_q],
                 e_far.at[own_q, h, pl.ds(4 * g, 4)],
                 h,
@@ -537,10 +553,10 @@
             df_copy(peer_c(n), n).wait_recv()
         dc_copy(core).start()
 
-    def backward(count, keys, vals, queries, e_of, factor, put):
+    def backward(count, keys_t, vals, queries, e_of, factor, put):
         dq = [[jnp.zeros((HALF, ROWS), F32) for h in range(2)] for _ in queries]
         for b in range(count):
-            k_t = keys(b).T
+            k_t = keys_t(b)
             val = vals(b)
             dk = jnp.zeros((ROWS, 128), F32)
             dv = jnp.zeros((ROWS, 128), F32)
@@ -564,7 +580,7 @@
 
         dq = backward(
             4,
-            lambda b: near_k[b],
+            lambda b: near_kt[b],
             lambda b: near_v[b],
             [j],
             lambda n, h, b: e_near[h, j, b],
@@ -641,7 +657,7 @@
 
         dq = backward(
             2,
-            lambda b: kv[in_z(dz, b), 0],
+            lambda b: kv[in_z(dz, b), 0].T,
             lambda b: kv[in_z(dz, b), 1],
             [4, 3],
             lambda n, h, b: e_far[n, h, 2 * i + b],
@@ -774,7 +790,11 @@
             pltpu.VMEM((4 * 128, 384), BF16),
             pltpu.VMEM((4, ROWS, 128), BF16),
             pltpu.VMEM((4, ROWS, 128), BF16),
+            pltpu.VMEM((4, 128, ROWS), BF16),
+            pltpu.VMEM((4, 128, ROWS), BF16),
             pltpu.VMEM((8, 2, ROWS, 128), BF16),
+            pltpu.VMEM((8, 128, ROWS), BF16),
+            pltpu.VMEM((RATE, ROWS, 128), BF16),
             pltpu.VMEM((2, 5, 128, ROWS), BF16),
             pltpu.VMEM((2, 5, ROWS, 128), BF16),
             pltpu.VMEM((2, 5, 128, ROWS), BF16),

time: 55.7 us -> 53.8 us (0.966)
  Pallas kernels: 54.9 us -> 52.7 us
    pallas_call x1, Pallas kernels: 52.7 us -> 50.5 us  [body(): pl.pallas_call(kernel, out_shape=(jax.ShapeDtypeStruct((128, WIDTH), BF16...]
where the time goes in v4:
time: 53.8 us; the launch traced here: 53.4 us
  Pallas kernels  52.7 us (98%)
  between operations  0.64 us (1%)
    pallas_call x1, Pallas kernels, body(): pl.pallas_call(kernel, out_shape=(jax.ShapeDtypeStruct((128, WIDTH), BF16...  50.5 us
    pallas_call x1, Pallas kernels, body(): pl.pallas_call(finish, out_shape=tuple((jax.ShapeDtypeStruct(r.shape, r.d...  2.2 us

profile of v4, /device:TPU:1, one launch (start us, length us, event | category | flops | bytes accessed | tf_op | source)
XLA Modules:
  0.0 53.4 jit_solution(5517869856127548861)
XLA Ops:
  0.6 50.5 %shard_map.110 = (bf16[128,768]{1,0:T(8,128)(2,1)}, bf16[256,384]{1,0:T(8,128)(2,1)}, bf16[256,384]{1,0:T(8,128)(2,1)}, bf16[256,384]{1,0:T(8,128)(2,1)}, bf16[96,768]{1,0:T(8,128)(2,1)}) custom-call(bf16[256,384]{1,0:T(8,128)(2,1)} %q_ref.1, bf16[256,384]{1,0:T(8,128)(2,1)} %k_ref.1, bf16[256,384]{1,0:T(8,128)(2,1)} %v_ref.1, s32[8,128]{1,0:T(8,128)} %bitcast.1, ...), custom_call_target="tpu_custom_call" | custom-call | flops 3000000000 | bytes 4000000 | tf_op jit(solution)/shard_map/pallas_call | solution.py:774
  51.2 2.2 %shard_map.111 = (bf16[128,768]{1,0:T(8,128)(2,1)}, bf16[256,384]{1,0:T(8,128)(2,1)}, bf16[256,384]{1,0:T(8,128)(2,1)}, bf16[256,384]{1,0:T(8,128)(2,1)}, bf16[96,768]{1,0:T(8,128)(2,1)}) custom-call(bf16[128,768]{1,0:T(8,128)(2,1)} %get-tuple-element.10.refs_0_, bf16[256,384]{1,0:T(8,128)(2,1)} %get-tuple-element.11.refs_1_, ...), custom_call_target="tpu_custom_call" | custom-call | tf_op jit(solution)/shard_map/pallas_call | solution.py:880

commit v5 on v4

--- a/solution.py
+++ b/solution.py
@@ -320,28 +320,35 @@
         q_t[0, j] = jnp.where(lane_col < HALF, q_jt, 0.0).astype(BF16)
         q_t[1, j] = jnp.where(lane_col < HALF, 0.0, q_jt).astype(BF16)
 
-    def forward(keys, vals_t, q_of, e_of, h):
-        top = None
+    halves = (slice(0, HALF), slice(HALF, 2 * HALF))
+
+    def forward(keys, vals_t, q_of, e_of):
+        top = [None, None]
         for b in range(4):
-            s = nn(keys(b), q_of)
-            e_of[b] = s
-            m = jnp.max(s, axis=0, keepdims=True)
-            top = m if top is None else jnp.maximum(top, m)
-        out = jnp.zeros((HALF, ROWS), F32)
+            for h in range(2):
+                s = nn(keys(b), q_of(h))
+                e_of(h)[b] = s
+                m = jnp.max(s, axis=0, keepdims=True)
+                top[h] = m if b == 0 else jnp.maximum(top[h], m)
+        out = [jnp.zeros((HALF, ROWS), F32), jnp.zeros((HALF, ROWS), F32)]
         for b in range(4):
-            e = jnp.exp2((e_of[b] - top) * EXP2)
-            e_of[b] = e
-            out = out + nn(vals_t(b)[h * HALF : (h + 1) * HALF], e.astype(BF16))
-        return top, out[HEAD : HEAD + 1], out
-
-    halves = (slice(0, HALF), slice(HALF, 2 * HALF))
+            for h in range(2):
+                e = jnp.exp2((e_of(h)[b] - top[h]) * EXP2)
+                e_of(h)[b] = e
+                out[h] = out[h] + nn(vals_t(b)[halves[h]], e.astype(BF16))
+        return [(top[h], out[h][HEAD : HEAD + 1], out[h]) for h in range(2)]
+
 
     @pl.loop(0, RATE)
     def _(j):
+        tiles = forward(
+            lambda b: near_k[b],
+            lambda b: near_vt[b],
+            lambda h: q_t[h, j],
+            lambda h: e_near.at[h, j],
+        )
         for h in range(2):
-            top, total, out = forward(
-                lambda b: near_k[b], lambda b: near_vt[b], q_t[h, j], e_near.at[h, j], h
-            )
+            top, total, out = tiles[h]
             top_n[h] = top
             sum_n[h] = total
             out_n[h] = out
@@ -410,14 +417,14 @@
             swap(1, m_far, m_got).start()
             swap(2, o_far, o_got).start()
 
+        tiles = forward(
+            lambda b: kv[far_block(4 * g + b), 0],
+            lambda b: far_vt[4 * g + b],
+            lambda h: q_t[h, 4 - own_q],
+            lambda h: e_far.at[own_q, h, pl.ds(4 * g, 4)],
+        )
         for h in range(2):
-            top, total, out = forward(
-                lambda b: kv[far_block(4 * g + b), 0],
-                lambda b: far_vt[4 * g + b],
-                q_t[h, 4 - own_q],
-                e_far.at[own_q, h, pl.ds(4 * g, 4)],
-                h,
-            )
+            top, total, out = tiles[h]
             top_f[own_q, h, g] = top
             sum_f[own_q, h, g] = total
             out_f[own_q, h, g] = out
@@ -555,18 +562,23 @@
 
     def backward(count, keys_t, vals, queries, e_of, factor, put):
         dq = [[jnp.zeros((HALF, ROWS), F32) for h in range(2)] for _ in queries]
+        pairs = [(n, h, j) for n, j in enumerate(queries) for h in range(2)]
+
+        def products(b):
+            return [nn(vals(b), g_t[h, j]) for _, h, j in pairs]
+
+        ahead = products(0)
         for b in range(count):
             k_t = keys_t(b)
-            val = vals(b)
+            now, ahead = ahead, products(b + 1) if b + 1 < count else None
             dk = jnp.zeros((ROWS, 128), F32)
             dv = jnp.zeros((ROWS, 128), F32)
-            for n, j in enumerate(queries):
-                for h in range(2):
-                    p = e_of(n, h, b) * factor(n, h)
-                    ds = (p * (nn(val, g_t[h, j]) - delta[h, j])).astype(BF16)
-                    dv = dv + nn(p.astype(BF16), g_n[h, j])
-                    dk = dk + nn(ds, q_n[h, j])
-                    dq[n][h] = dq[n][h] + nn(k_t[halves[h]], ds)
+            for (n, h, j), d_prob in zip(pairs, now, strict=True):
+                p = e_of(n, h, b) * factor(n, h)
+                ds = (p * (d_prob - delta[h, j])).astype(BF16)
+                dv = dv + nn(p.astype(BF16), g_n[h, j])
+                dk = dk + nn(ds, q_n[h, j])
+                dq[n][h] = dq[n][h] + nn(k_t[halves[h]], ds)
             put(b, dk, dv)
         return dq
 

time: 53.8 us -> 52.3 us (0.972)
  Pallas kernels: 52.7 us -> 50.9 us
    pallas_call x1, Pallas kernels: 50.5 us -> 48.6 us  [body(): pl.pallas_call(kernel, out_shape=(jax.ShapeDtypeStruct((128, WIDTH), BF16...]
where the time goes in v5:
time: 52.3 us; the launch traced here: 51.5 us
  Pallas kernels  50.9 us (97%)
  between operations  0.64 us (1%)
    pallas_call x1, Pallas kernels, body(): pl.pallas_call(kernel, out_shape=(jax.ShapeDtypeStruct((128, WIDTH), BF16...  48.6 us
    pallas_call x1, Pallas kernels, body(): pl.pallas_call(finish, out_shape=tuple((jax.ShapeDtypeStruct(r.shape, r.d...  2.2 us

profile of v5, /device:TPU:1, one launch (start us, length us, event | category | flops | bytes accessed | tf_op | source)
XLA Modules:
  0.0 51.5 jit_solution(14397840483491111465)
XLA Ops:
  0.6 48.6 %shard_map.110 = (bf16[128,768]{1,0:T(8,128)(2,1)}, bf16[256,384]{1,0:T(8,128)(2,1)}, bf16[256,384]{1,0:T(8,128)(2,1)}, bf16[256,384]{1,0:T(8,128)(2,1)}, bf16[96,768]{1,0:T(8,128)(2,1)}) custom-call(bf16[256,384]{1,0:T(8,128)(2,1)} %q_ref.1, bf16[256,384]{1,0:T(8,128)(2,1)} %k_ref.1, bf16[256,384]{1,0:T(8,128)(2,1)} %v_ref.1, s32[8,128]{1,0:T(8,128)} %bitcast.1, ...), custom_call_target="tpu_custom_call" | custom-call | flops 3000000000 | bytes 4000000 | tf_op jit(solution)/shard_map/pallas_call | solution.py:786
  49.3 2.2 %shard_map.111 = (bf16[128,768]{1,0:T(8,128)(2,1)}, bf16[256,384]{1,0:T(8,128)(2,1)}, bf16[256,384]{1,0:T(8,128)(2,1)}, bf16[256,384]{1,0:T(8,128)(2,1)}, bf16[96,768]{1,0:T(8,128)(2,1)}) custom-call(bf16[128,768]{1,0:T(8,128)(2,1)} %get-tuple-element.10.refs_0_, bf16[256,384]{1,0:T(8,128)(2,1)} %get-tuple-element.11.refs_1_, ...), custom_call_target="tpu_custom_call" | custom-call | tf_op jit(solution)/shard_map/pallas_call | solution.py:892

commit v6 on v5

--- a/solution.py
+++ b/solution.py
@@ -322,41 +322,41 @@
 
     halves = (slice(0, HALF), slice(HALF, 2 * HALF))
 
-    def forward(keys, vals_t, q_of, e_of):
-        top = [None, None]
+    def forward(keys, vals_t, chains, q_of, e_of):
+        top = {}
         for b in range(4):
-            for h in range(2):
-                s = nn(keys(b), q_of(h))
-                e_of(h)[b] = s
+            for c in chains:
+                s = nn(keys(b), q_of(*c))
+                e_of(*c)[b] = s
                 m = jnp.max(s, axis=0, keepdims=True)
-                top[h] = m if b == 0 else jnp.maximum(top[h], m)
-        out = [jnp.zeros((HALF, ROWS), F32), jnp.zeros((HALF, ROWS), F32)]
+                top[c] = m if b == 0 else jnp.maximum(top[c], m)
+        out = {c: jnp.zeros((HALF, ROWS), F32) for c in chains}
         for b in range(4):
-            for h in range(2):
-                e = jnp.exp2((e_of(h)[b] - top[h]) * EXP2)
-                e_of(h)[b] = e
-                out[h] = out[h] + nn(vals_t(b)[halves[h]], e.astype(BF16))
-        return [(top[h], out[h][HEAD : HEAD + 1], out[h]) for h in range(2)]
-
-
-    @pl.loop(0, RATE)
-    def _(j):
+            for c in chains:
+                e = jnp.exp2((e_of(*c)[b] - top[c]) * EXP2)
+                e_of(*c)[b] = e
+                out[c] = out[c] + nn(vals_t(b)[halves[c[1]]], e.astype(BF16))
+        return {c: (top[c], out[c][HEAD : HEAD + 1], out[c]) for c in chains}
+
+    @pl.loop(0, 2)
+    def _(pair):
         tiles = forward(
             lambda b: near_k[b],
             lambda b: near_vt[b],
-            lambda h: q_t[h, j],
-            lambda h: e_near.at[h, j],
+            [(d, h) for d in range(2) for h in range(2)],
+            lambda d, h: q_t[h, 2 * pair + d],
+            lambda d, h: e_near.at[h, 2 * pair + d],
         )
-        for h in range(2):
-            top, total, out = tiles[h]
-            top_n[h] = top
-            sum_n[h] = total
-            out_n[h] = out
+        for (d, h), (top, total, out) in tiles.items():
+            if d == 1:
+                top_n[h] = top
+                sum_n[h] = total
+                out_n[h] = out
             inverse = 1.0 / total
-            fac_n[h, j] = inverse
-            attn_t[j, halves[h]] = (out * inverse).astype(BF16)
-
-        @pl.when(j == 0)
+            fac_n[h, 2 * pair + d] = inverse
+            attn_t[2 * pair + d, halves[h]] = (out * inverse).astype(BF16)
+
+        @pl.when(pair == 0)
         def _():
             dy_copy(partner_h, 0, partner_h).wait_recv()
             for n, turn in enumerate((1, 3)):
@@ -420,11 +420,11 @@
         tiles = forward(
             lambda b: kv[far_block(4 * g + b), 0],
             lambda b: far_vt[4 * g + b],
-            lambda h: q_t[h, 4 - own_q],
-            lambda h: e_far.at[own_q, h, pl.ds(4 * g, 4)],
+            [(0, h) for h in range(2)],
+            lambda d, h: q_t[h, 4 - own_q],
+            lambda d, h: e_far.at[own_q, h, pl.ds(4 * g, 4)],
         )
-        for h in range(2):
-            top, total, out = tiles[h]
+        for (_, h), (top, total, out) in tiles.items():
             top_f[own_q, h, g] = top
             sum_f[own_q, h, g] = total
             out_f[own_q, h, g] = out

time: 52.3 us -> 50.8 us (0.971)
  Pallas kernels: 50.9 us -> 49.4 us
    pallas_call x1, Pallas kernels: 48.6 us -> 47.2 us  [body(): pl.pallas_call(kernel, out_shape=(jax.ShapeDtypeStruct((128, WIDTH), BF16...]
where the time goes in v6:
time: 50.8 us; the launch traced here: 50 us
  Pallas kernels  49.4 us (97%)
  between operations  0.64 us (1%)
    pallas_call x1, Pallas kernels, body(): pl.pallas_call(kernel, out_shape=(jax.ShapeDtypeStruct((128, WIDTH), BF16...  47.2 us
    pallas_call x1, Pallas kernels, body(): pl.pallas_call(finish, out_shape=tuple((jax.ShapeDtypeStruct(r.shape, r.d...  2.2 us

profile of v6, /device:TPU:1, one launch (start us, length us, event | category | flops | bytes accessed | tf_op | source)
XLA Modules:
  0.0 50.0 jit_solution(14504400465574342770)
XLA Ops:
  0.6 47.2 %shard_map.110 = (bf16[128,768]{1,0:T(8,128)(2,1)}, bf16[256,384]{1,0:T(8,128)(2,1)}, bf16[256,384]{1,0:T(8,128)(2,1)}, bf16[256,384]{1,0:T(8,128)(2,1)}, bf16[96,768]{1,0:T(8,128)(2,1)}) custom-call(bf16[256,384]{1,0:T(8,128)(2,1)} %q_ref.1, bf16[256,384]{1,0:T(8,128)(2,1)} %k_ref.1, bf16[256,384]{1,0:T(8,128)(2,1)} %v_ref.1, s32[8,128]{1,0:T(8,128)} %bitcast.1, ...), custom_call_target="tpu_custom_call" | custom-call | flops 3000000000 | bytes 4000000 | tf_op jit(solution)/shard_map/pallas_call | solution.py:786
  47.8 2.2 %shard_map.111 = (bf16[128,768]{1,0:T(8,128)(2,1)}, bf16[256,384]{1,0:T(8,128)(2,1)}, bf16[256,384]{1,0:T(8,128)(2,1)}, bf16[256,384]{1,0:T(8,128)(2,1)}, bf16[96,768]{1,0:T(8,128)(2,1)}) custom-call(bf16[128,768]{1,0:T(8,128)(2,1)} %get-tuple-element.10.refs_0_, bf16[256,384]{1,0:T(8,128)(2,1)} %get-tuple-element.11.refs_1_, ...), custom_call_target="tpu_custom_call" | custom-call | tf_op jit(solution)/shard_map/pallas_call | solution.py:892

commit v7 on v6

--- a/solution.py
+++ b/solution.py
@@ -391,12 +391,9 @@
 
     turn_values(0)
 
-    @pl.loop(0, 4)
-    def _(step):
-        g = lax.rem(step, 2)
-        own_q = step // 2
-
-        @pl.when(step == 1)
+    @pl.loop(0, 2)
+    def _(g):
+        @pl.when(g == 1)
         def _():
             for i in (2, 3):
                 share(i)
@@ -404,30 +401,28 @@
                 kv_copy(in_z(dz, 1 - core), 0, partner).wait_recv()
             turn_values(1)
 
-        @pl.when(step == 2)
-        def _():
-            for h in range(2):
-                top = jnp.maximum(top_f[0, h, 0], top_f[0, h, 1])
-                w0 = jnp.exp2((top_f[0, h, 0] - top) * EXP2)
-                w1 = jnp.exp2((top_f[0, h, 1] - top) * EXP2)
-                m_far[h : h + 1] = top
-                m_far[2 + h : 3 + h] = w0 * sum_f[0, h, 0] + w1 * sum_f[0, h, 1]
-                o_far[halves[h]] = (w0 * out_f[0, h, 0] + w1 * out_f[0, h, 1]).astype(BF16)
-            m_far[4:8] = jnp.zeros((4, ROWS), F32)
-            swap(1, m_far, m_got).start()
-            swap(2, o_far, o_got).start()
-
         tiles = forward(
             lambda b: kv[far_block(4 * g + b), 0],
             lambda b: far_vt[4 * g + b],
-            [(0, h) for h in range(2)],
-            lambda d, h: q_t[h, 4 - own_q],
-            lambda d, h: e_far.at[own_q, h, pl.ds(4 * g, 4)],
+            [(d, h) for d in range(2) for h in range(2)],
+            lambda d, h: q_t[h, 4 - d],
+            lambda d, h: e_far.at[d, h, pl.ds(4 * g, 4)],
         )
-        for (_, h), (top, total, out) in tiles.items():
-            top_f[own_q, h, g] = top
-            sum_f[own_q, h, g] = total
-            out_f[own_q, h, g] = out
+        for (d, h), (top, total, out) in tiles.items():
+            top_f[d, h, g] = top
+            sum_f[d, h, g] = total
+            out_f[d, h, g] = out
+
+    for h in range(2):
+        top = jnp.maximum(top_f[0, h, 0], top_f[0, h, 1])
+        w0 = jnp.exp2((top_f[0, h, 0] - top) * EXP2)
+        w1 = jnp.exp2((top_f[0, h, 1] - top) * EXP2)
+        m_far[h : h + 1] = top
+        m_far[2 + h : 3 + h] = w0 * sum_f[0, h, 0] + w1 * sum_f[0, h, 1]
+        o_far[halves[h]] = (w0 * out_f[0, h, 0] + w1 * out_f[0, h, 1]).astype(BF16)
+    m_far[4:8] = jnp.zeros((4, ROWS), F32)
+    swap(1, m_far, m_got).start()
+    swap(2, o_far, o_got).start()
 
     for turn in (1, 3):
         for x in range(2):

time: 50.8 us -> 51.2 us (level)
    pallas_call x1, Pallas kernels: 47.2 us -> 47.7 us  [body(): pl.pallas_call(kernel, out_shape=(jax.ShapeDtypeStruct((128, WIDTH), BF16...]
where the time goes in v7:
time: 51.2 us; the launch traced here: 50.5 us
  Pallas kernels  49.9 us (97%)
  between operations  0.64 us (1%)
    pallas_call x1, Pallas kernels, body(): pl.pallas_call(kernel, out_shape=(jax.ShapeDtypeStruct((128, WIDTH), BF16...  47.7 us
    pallas_call x1, Pallas kernels, body(): pl.pallas_call(finish, out_shape=tuple((jax.ShapeDtypeStruct(r.shape, r.d...  2.2 us

profile of v7, /device:TPU:1, one launch (start us, length us, event | category | flops | bytes accessed | tf_op | source)
XLA Modules:
  0.0 50.5 jit_solution(11762083298677360337)
XLA Ops:
  0.6 47.7 %shard_map.110 = (bf16[128,768]{1,0:T(8,128)(2,1)}, bf16[256,384]{1,0:T(8,128)(2,1)}, bf16[256,384]{1,0:T(8,128)(2,1)}, bf16[256,384]{1,0:T(8,128)(2,1)}, bf16[96,768]{1,0:T(8,128)(2,1)}) custom-call(bf16[256,384]{1,0:T(8,128)(2,1)} %q_ref.1, bf16[256,384]{1,0:T(8,128)(2,1)} %k_ref.1, bf16[256,384]{1,0:T(8,128)(2,1)} %v_ref.1, s32[8,128]{1,0:T(8,128)} %bitcast.1, ...), custom_call_target="tpu_custom_call" | custom-call | flops 3000000000 | bytes 4000000 | tf_op jit(solution)/shard_map/pallas_call | solution.py:781
  48.3 2.2 %shard_map.111 = (bf16[128,768]{1,0:T(8,128)(2,1)}, bf16[256,384]{1,0:T(8,128)(2,1)}, bf16[256,384]{1,0:T(8,128)(2,1)}, bf16[256,384]{1,0:T(8,128)(2,1)}, bf16[96,768]{1,0:T(8,128)(2,1)}) custom-call(bf16[128,768]{1,0:T(8,128)(2,1)} %get-tuple-element.10.refs_0_, bf16[256,384]{1,0:T(8,128)(2,1)} %get-tuple-element.11.refs_1_, ...), custom_call_target="tpu_custom_call" | custom-call | tf_op jit(solution)/shard_map/pallas_call | solution.py:887
